TPU v7x, 128 devices: a whole 4x4x4 slice. The times are simulated.
128 devices in a mesh: dom: 128 (over z, y, x, core).
Axes of the slice: x: 4, y: 4, z: 4, core: 2. Of those that a mesh axis runs over, the one named last changes fastest.
Arguments:
- fine_state: float32 [20, 9, 16384], P(None, None, 'dom'), may hold values from -6 to 6
- coarse_state: float32 [20, 9, 32768], P(None, None, 'dom'), may hold values from -6 to 6
- fine_star: float32 [3, 9, 9, 16384], P(None, None, None, 'dom'), may hold values from -2 to 2
- coarse_star: float32 [3, 9, 9, 32768], P(None, None, None, 'dom'), may hold values from -2 to 2
- fine_flux: float32 [2, 4, 9, 9, 16384], P(None, None, None, None, 'dom'), may hold values from -2 to 2
- coarse_flux: float32 [2, 4, 9, 9, 32768], P(None, None, None, None, 'dom'), may hold values from -2 to 2
- fine_neighbors: int32 [4, 16384], P(None, 'dom'), may hold values from 0 to 527
- fine_faces: int32 [4, 16384], P(None, 'dom'), may hold values from 0 to 3
- fine_turns: int32 [4, 16384], P(None, 'dom'), may hold values from 0 to 2
- coarse_neighbors: int32 [4, 32768], P(None, 'dom'), may hold values from 0 to 527
- coarse_faces: int32 [4, 32768], P(None, 'dom'), may hold values from 0 to 3
- coarse_turns: int32 [4, 32768], P(None, 'dom'), may hold values from 0 to 2
- fine_count: int32 [128], P('dom'), may hold values from 1 to 128, 8192 in all
- send_fine: int32 [128, 12, 8], P('dom'), may hold values from 0 to 127
- send_coarse: int32 [128, 12, 4], P('dom'), may hold values from 0 to 255
- stiff_time: float32 [3, 20, 20], replicated, may hold values from -1.25 to 1.25
- stiff_volume: float32 [3, 20, 20], replicated, may hold values from -1.25 to 1.25
- face_lift: float32 [4, 20, 6], replicated, may hold values from -2.5 to 2.5
- face_project: float32 [4, 6, 20], replicated, may hold values from -1.25 to 1.25
- face_rotate: float32 [3, 6, 6], replicated, may hold values from -2.5 to 2.5
Outputs:
- fine_result: float32 [20, 9, 16384], P(None, None, 'dom')
- coarse_result: float32 [20, 9, 32768], P(None, None, 'dom')
Inputs may be any that keep to these rules, and one draw needn't show every extreme that they name: `fine_count`: fine elements occupy the leading slots of each block; some block is full. `fine_neighbors`: indices into the partition's neighbour table of 528 entries. `coarse_neighbors`: indices into the partition's neighbour table of 528 entries. `send_fine`: local fine slot numbers of the sending partition. `send_coarse`: local coarse element numbers of the sending partition.
All inputs are finite; a program needn't handle non-finite values.
Results may differ from a plain program's by a relative error of at most 0.0001.
Values sent between devices are 32-bit elements; how exact they have to be, the bound alone decides.
No kernel may reach another device: no remote copies, remote signals or barrier semaphores. Data moves between devices by JAX's collectives and lax.ppermute only.
A program may use at most 128 MiB of HBM per device.

v0:
```python
from functools import partial

import jax
import jax.numpy as jnp
from jax import lax
from jax.experimental import pallas as pl
from jax.experimental.pallas import tpu as pltpu
from jax.sharding import PartitionSpec as P

NB = 20
NQ = 9
FNB = 6
REACH = 6
BP = 24
FP = 8
LANES = 128
ROW = 384
FIRST_HALF = (0.5, 0.125, 1.0 / 48.0)
SECOND_HALF = (0.5, 0.375, 7.0 / 48.0)
F32 = jnp.float32
BF16 = jnp.bfloat16
I32 = jnp.int32
N_DEV = 128


def halves(x):
    hi = x.astype(BF16).astype(F32)
    return hi, x - hi


def stacked(x):
    hi, lo = halves(x)
    return jnp.concatenate([hi, lo, hi], axis=0).astype(BF16)


def fill_weight(ref, blocks, row_step, col_step):
    ref[...] = jnp.zeros(ref.shape, F32)
    for i, block in enumerate(blocks):
        rows, cols = block.shape
        hi, lo = halves(block)
        span = slice(i * row_step, i * row_step + rows)
        ref[span, 0:cols] = hi
        ref[span, col_step : col_step + cols] = hi
        ref[span, 2 * col_step : 2 * col_step + cols] = lo


def weight(ref, depth):
    return ref[:, 0 : 3 * depth].astype(BF16)


def mm(w, x):
    return jnp.dot(w, stacked(x), preferred_element_type=F32)


def load_state(state_ref, x_ref, width):
    for q in range(NQ):
        x_ref[NB:BP, q * width : (q + 1) * width] = jnp.zeros((BP - NB, width), F32)
        x_ref[0:NB, q * width : (q + 1) * width] = state_ref[:, q, :]


def star_sum(t_ref, star_ref, width, tile):
    lanes = slice(tile * LANES, (tile + 1) * LANES)
    acc = [None] * NQ
    for d in range(3):
        for q in range(NQ):
            t = t_ref[d * BP : (d + 1) * BP, q * width + tile * LANES : q * width + (tile + 1) * LANES]
            for p in range(NQ):
                term = t * star_ref[d, q, p : p + 1, lanes]
                acc[p] = term if acc[p] is None else acc[p] + term
    return acc


def put(ref, values, width, tile):
    for p in range(NQ):
        ref[:, p * width + tile * LANES : p * width + (tile + 1) * LANES] = values[p]


def get(ref, width, tile):
    return [
        ref[:, p * width + tile * LANES : p * width + (tile + 1) * LANES] for p in range(NQ)
    ]


def predictor(x_ref, d_ref, t_ref, star_ref, w, width, emit):
    tiles = width // LANES
    t_ref[...] = mm(w, x_ref[...])
    for tile in range(tiles):
        put(d_ref, star_sum(t_ref, star_ref, width, tile), width, tile)
    t_ref[...] = mm(w, d_ref[...])
    for tile in range(tiles):
        second = star_sum(t_ref, star_ref, width, tile)
        emit(tile, get(x_ref, width, tile), get(d_ref, width, tile), second)


def combine(weights, state, neg_first, second):
    return [
        weights[0] * s - weights[1] * f + weights[2] * g
        for s, f, g in zip(state, neg_first, second)
    ]


def place():
    me = lax.axis_index("dom").astype(I32)
    return me, me >> 1, me & 1


def route(plane, pos, rel):
    me, chip, core = place()
    even = ((chip >> 3) << 3) + pos
    odd = (((chip + 4) >> 3) << 3) - 4 + ((pos + 4) & 7)
    target = jnp.where(plane == 0, even, odd)
    cross = (target >> 3) != (chip >> 3)
    other = (rel ^ plane)
    offset = 2 * (target - chip) + other - core
    valid = (target >= 0) & (target < N_DEV // 2) & (offset >= -REACH) & (offset <= REACH)
    valid = valid & (offset != 0) & ((plane == 0) | cross)
    peer = jnp.where(offset < 0, offset + REACH, offset + REACH - 1)
    return jnp.clip(peer, 0, 2 * REACH - 1), valid


def picker(send_ref, plane, width, slots):
    rows = []
    for m in range(16):
        peer, valid = route(plane, m // 2, m % 2)
        row = send_ref[0, pl.ds(peer, 1), :]
        rows.append(jnp.broadcast_to(jnp.where(valid, row, -1), (8, width)))
    big = jnp.concatenate(rows, axis=0).astype(F32)
    s = lax.broadcasted_iota(I32, (LANES, width), 0) & (width - 1)
    lane = lax.broadcasted_iota(I32, (LANES, width), 1)
    index = jnp.sum(jnp.where(lane == s, big, 0.0), axis=1, keepdims=True)
    slot = lax.broadcasted_iota(I32, (LANES, slots), 1).astype(F32)
    return jnp.where(slot == index, 1.0, 0.0).astype(BF16)


def rows_of(ref, width, first, last):
    return jnp.concatenate([ref[:, q * width : (q + 1) * width] for q in range(first, last)], axis=0)


def picked(hot, field):
    hi, lo = halves(field)
    both = jnp.concatenate([hi, lo], axis=1).astype(BF16)
    hots = jnp.concatenate([hot, hot], axis=1)
    return lax.dot_general(hots, both, (((1,), (1,)), ((), ())), preferred_element_type=F32)


def pack(out_ref, plane, fine_ref, coarse_ref, send_fine_ref, send_coarse_ref):
    hot = picker(send_fine_ref, plane, 8, LANES)
    out_ref[:, 0:256] = jnp.zeros((LANES, 256), F32)
    out_ref[:, 0 : NQ * BP] = picked(hot, rows_of(fine_ref, LANES, 0, NQ))
    hot = picker(send_coarse_ref, plane, 4, 2 * LANES)
    low = picked(hot, rows_of(coarse_ref, 2 * LANES, 0, 5))
    high = picked(hot, rows_of(coarse_ref, 2 * LANES, 5, NQ))
    high = jnp.concatenate([high, jnp.zeros((LANES, BP), F32)], axis=1)
    s = lax.broadcasted_iota(I32, (LANES, 5 * BP), 0) & 7
    out_ref[:, 256:ROW] = jnp.zeros((LANES, LANES), F32)
    out_ref[:, 256 : 256 + 5 * BP] = jnp.where(s < 4, low, high)


def unpack(mine_ref, back_ref, prior, fine_ref, coarse_ref):
    parts = []
    for i in range(8):
        for rel in range(2):
            parts.append(mine_ref[i, rel, 0] + back_ref[i, 1 - rel])
    rows = jnp.concatenate(parts, axis=0)
    turned = [rows[:, t * LANES : (t + 1) * LANES].T for t in range(3)]
    fine = jnp.concatenate(turned[:2], axis=0)
    coarse = turned[2]
    for q in range(NQ):
        fine_ref[:, q * LANES : (q + 1) * LANES] = fine[q * BP : (q + 1) * BP]
        at = (q % 5) * BP
        coarse_ref[:, q * LANES : (q + 1) * LANES] = coarse[at : at + BP]


def first_kernel(
    fine_state, fine_star, coarse_state, coarse_star, count, send_fine, send_coarse, stiff,
    keep, swap, x_fine, i_fine, x_coarse, c_first, c_second,
    w_ref, d_fine, t_fine, d_coarse, t_coarse,
):
    fill_weight(w_ref, [stiff[d] for d in range(3)], BP, BP)
    w = weight(w_ref, BP)
    load_state(coarse_state, x_coarse, 2 * LANES)
    load_state(fine_state, x_fine, LANES)

    def emit_coarse(tile, *terms):
        put(c_first, combine(FIRST_HALF, *terms), 2 * LANES, tile)
        put(c_second, combine(SECOND_HALF, *terms), 2 * LANES, tile)

    live = lax.broadcasted_iota(I32, (BP, LANES), 1) < count[0]

    def emit_fine(tile, *terms):
        values = combine(FIRST_HALF, *terms)
        put(i_fine, [jnp.where(live, v, 0.0) for v in values], LANES, tile)

    predictor(x_coarse, d_coarse, t_coarse, coarse_star, w, 2 * LANES, emit_coarse)
    predictor(x_fine, d_fine, t_fine, fine_star, w, LANES, emit_fine)
    core = place()[2]
    pack(keep, core, i_fine, c_first, send_fine, send_coarse)
    pack(swap, 1 - core, i_fine, c_first, send_fine, send_coarse)


def locate(n):
    me, _, core = place()
    local = n < 384
    fine = n < 480
    g = jnp.where(fine, n - 384, n - 480)
    j = jnp.where(fine, g >> 3, g >> 2)
    s = jnp.where(fine, g & 7, g & 3)
    offset = j - REACH + jnp.where(j >= REACH, 1, 0)
    block = ((me - offset) & 15) ^ core
    lane = jnp.where(local, n & 127, block * 8 + s)
    tile = jnp.where(local, n >> 7, jnp.where(fine, 3, 4))
    return tile, lane


def correct(
    state_ref, i_ref, width, tables, neighbors, faces, turns, star_ref, flux_ref, weights,
    p_ref, t_ref, n_ref, l_ref, emit,
):
    w_vol, w_proj, w_rot, w_lift = weights
    p_ref[...] = mm(w_proj, i_ref[...])
    t_ref[...] = mm(w_vol, i_ref[...])
    for tile in range(width // LANES):
        lanes = slice(tile * LANES, (tile + 1) * LANES)
        for i in range(4):
            number = jnp.broadcast_to(neighbors[i : i + 1, lanes], (8, LANES))
            where_tile, lane = locate(number)
            later = jnp.where(where_tile == 4, lane + 4, lane)
            masks = [where_tile == k for k in range(5)]
            for q in range(NQ):
                at = lane if q < 5 else later
                for g in range(3):
                    value = None
                    for k, (ref, ref_width, ref_tile) in enumerate(tables):
                        start = q * ref_width + ref_tile * LANES
                        source = ref[8 * g : 8 * g + 8, start : start + LANES]
                        found = jnp.take_along_axis(source, at, axis=1)
                        value = found if value is None else jnp.where(masks[k], found, value)
                    n_ref[8 * g : 8 * g + 8, q * LANES : (q + 1) * LANES] = value
            projected = mm(w_proj, n_ref[...])
            face = jnp.broadcast_to(faces[i : i + 1, lanes], (FP, LANES))
            turn = jnp.broadcast_to(turns[i : i + 1, lanes], (FP, LANES))
            chosen = []
            for q in range(NQ):
                at = slice(q * LANES, (q + 1) * LANES)
                value = projected[0:FP, at]
                for f in range(1, 4):
                    value = jnp.where(face == f, projected[f * FP : (f + 1) * FP, at], value)
                chosen.append(value)
            rotated = mm(w_rot, jnp.concatenate(chosen, axis=1))
            acc = [None] * NQ
            for q in range(NQ):
                at = slice(q * LANES, (q + 1) * LANES)
                other = rotated[0:FP, at]
                for h in range(1, 3):
                    other = jnp.where(turn == h, rotated[h * FP : (h + 1) * FP, at], other)
                start = q * width + tile * LANES
                own = p_ref[i * FP : (i + 1) * FP, start : start + LANES]
                for p in range(NQ):
                    term = own * flux_ref[0, i, q, p : p + 1, lanes]
                    term = term + other * flux_ref[1, i, q, p : p + 1, lanes]
                    acc[p] = term if acc[p] is None else acc[p] + term
            for p in range(NQ):
                l_ref[i * FP : (i + 1) * FP, p * LANES : (p + 1) * LANES] = acc[p]
        lifted = mm(w_lift, l_ref[...])
        volume = star_sum(t_ref, star_ref, width, tile)
        state = get(state_ref, width, tile)
        emit(
            tile,
            [state[p] + (volume[p] + lifted[:, p * LANES : (p + 1) * LANES]) for p in range(NQ)],
        )


def fill_corrector(stiff_volume, lift, project, rotate, w_vol, w_proj, w_rot, w_lift):
    fill_weight(w_vol, [stiff_volume[d] for d in range(3)], BP, BP)
    fill_weight(w_proj, [project[f] for f in range(4)], FP, BP)
    fill_weight(w_rot, [rotate[h] for h in range(3)], FP, FP)
    w_lift[...] = jnp.zeros(w_lift.shape, F32)
    for i in range(4):
        hi, lo = halves(lift[i])
        w_lift[0:NB, i * FP : i * FP + FNB] = hi
        w_lift[0:NB, 32 + i * FP : 32 + i * FP + FNB] = hi
        w_lift[0:NB, 64 + i * FP : 64 + i * FP + FNB] = lo
    return weight(w_vol, BP), weight(w_proj, BP), weight(w_rot, FP), weight(w_lift, 32)


def second_kernel(
    mine, back, x_fine, i_fine, c_first, c_second, fine_star, fine_flux,
    neighbors, faces, turns, count, send_fine, send_coarse,
    stiff, stiff_volume, lift, project, rotate,
    keep, swap, x_next, i_next, ghost_f, ghost_c,
    w_ref, w_vol, w_proj, w_rot, w_lift, p_ref, t_ref, n_ref, l_ref, d_ref,
):
    weights = fill_corrector(stiff_volume, lift, project, rotate, w_vol, w_proj, w_rot, w_lift)
    fill_weight(w_ref, [stiff[d] for d in range(3)], BP, BP)
    unpack(mine, back, None, ghost_f, ghost_c)
    live = lax.broadcasted_iota(I32, (BP, LANES), 1) < count[0]
    tables = [
        (i_fine, LANES, 0), (c_first, 2 * LANES, 0), (c_first, 2 * LANES, 1),
        (ghost_f, LANES, 0), (ghost_c, LANES, 0),
    ]

    def emit_state(tile, values):
        old = get(x_fine, LANES, 0)
        put(x_next, [jnp.where(live, v, o) for v, o in zip(values, old)], LANES, 0)

    correct(
        x_fine, i_fine, LANES, tables, neighbors, faces, turns, fine_star, fine_flux, weights,
        p_ref, t_ref, n_ref, l_ref, emit_state,
    )

    def emit_fine(tile, *terms):
        values = combine(FIRST_HALF, *terms)
        put(i_next, [jnp.where(live, v, 0.0) for v in values], LANES, 0)

    predictor(x_next, d_ref, t_ref, fine_star, weight(w_ref, BP), LANES, emit_fine)
    core = place()[2]
    pack(keep, core, i_next, c_second, send_fine, send_coarse)
    pack(swap, 1 - core, i_next, c_second, send_fine, send_coarse)


def third_kernel(
    mine, back, x_fine, i_first, i_fine, x_coarse, c_first, c_second, g_fine, g_coarse,
    fine_star, fine_flux, coarse_star, coarse_flux,
    neighbors, faces, turns, c_neighbors, c_faces, c_turns, count,
    stiff_volume, lift, project, rotate,
    fine_out, coarse_out,
    w_vol, w_proj, w_rot, w_lift, p_ref, t_ref, n_ref, l_ref, pc_ref, tc_ref,
    ghost_f, ghost_c, c_full, i_both,
):
    weights = fill_corrector(stiff_volume, lift, project, rotate, w_vol, w_proj, w_rot, w_lift)
    unpack(mine, back, None, ghost_f, ghost_c)
    live = lax.broadcasted_iota(I32, (NB, LANES), 1) < count[0]
    tables = [
        (i_fine, LANES, 0), (c_second, 2 * LANES, 0), (c_second, 2 * LANES, 1),
        (ghost_f, LANES, 0), (ghost_c, LANES, 0),
    ]

    def emit_fine(tile, values):
        old = get(x_fine, LANES, 0)
        for p in range(NQ):
            fine_out[:, p, :] = jnp.where(live, values[p][:NB], old[p][:NB])

    correct(
        x_fine, i_fine, LANES, tables, neighbors, faces, turns, fine_star, fine_flux, weights,
        p_ref, t_ref, n_ref, l_ref, emit_fine,
    )
    c_full[...] = c_first[...] + c_second[...]
    i_both[...] = i_first[...] + i_fine[...]
    ghost_f[...] = ghost_f[...] + g_fine[...]
    ghost_c[...] = ghost_c[...] + g_coarse[...]
    tables = [
        (i_both, LANES, 0), (c_full, 2 * LANES, 0), (c_full, 2 * LANES, 1),
        (ghost_f, LANES, 0), (ghost_c, LANES, 0),
    ]

    def emit_coarse(tile, values):
        for p in range(NQ):
            coarse_out[:, p, tile * LANES : (tile + 1) * LANES] = values[p][:NB]

    correct(
        x_coarse, c_full, 2 * LANES, tables, c_neighbors, c_faces, c_turns, coarse_star,
        coarse_flux, weights, pc_ref, tc_ref, n_ref, l_ref, emit_coarse,
    )


VM = pl.BlockSpec(memory_space=pltpu.VMEM)
SM = pl.BlockSpec(memory_space=pltpu.SMEM)


def struct(*shape):
    return jax.ShapeDtypeStruct(shape, F32)


def scratch(*shape):
    return pltpu.VMEM(shape, F32)


FINE = (BP, NQ * LANES)
COARSE = (BP, 2 * NQ * LANES)
SENT = (LANES, ROW)
WEIGHTS = [(3 * BP, LANES), (4 * FP, LANES), (3 * FP, LANES), (BP, LANES)]
PARAMS = pltpu.CompilerParams(vmem_limit_bytes=24 * 1024 * 1024)


def call(kernel, name, in_specs, outs, scratches, args):
    return pl.pallas_call(
        kernel,
        name=name,
        in_specs=in_specs,
        out_specs=[VM] * len(outs),
        out_shape=[struct(*s) for s in outs],
        scratch_shapes=[scratch(*s) for s in scratches],
        compiler_params=PARAMS,
    )(*args)


def planes():
    groups = []
    for core in range(2):
        for k in range(8):
            first = [8 * k + i for i in range(8)]
            second = [(8 * k - 4 + (i + 4) % 8) % 64 for i in range(8)]
            groups.append([2 * chip + core for chip in (second if core else first)])
    return groups


SIBLING = [(i, i ^ 1) for i in range(N_DEV)]


def exchange(keep, swap):
    arrived = lax.ppermute(swap, "dom", SIBLING)
    blocks = jnp.stack([keep.reshape(8, 2, 8, ROW), arrived.reshape(8, 2, 8, ROW)], axis=1)
    got = lax.all_to_all(blocks, "dom", 0, 0, axis_index_groups=planes(), tiled=True)
    back = lax.ppermute(got[:, :, 1], "dom", SIBLING)
    return got, back


def local(
    fine_state, coarse_state, fine_star, coarse_star, fine_flux, coarse_flux,
    fine_neighbors, fine_faces, fine_turns, coarse_neighbors, coarse_faces, coarse_turns,
    fine_count, send_fine, send_coarse,
    stiff_time, stiff_volume, face_lift, face_project, face_rotate,
):
    keep, swap, x_fine, i_first, x_coarse, c_first, c_second = call(
        first_kernel, "predict",
        [VM, VM, VM, VM, SM, VM, VM, VM],
        [SENT, SENT, FINE, FINE, COARSE, COARSE, COARSE],
        [(3 * BP, LANES), FINE, (3 * BP, NQ * LANES), COARSE, (3 * BP, 2 * NQ * LANES)],
        (fine_state, fine_star, coarse_state, coarse_star, fine_count, send_fine, send_coarse,
         stiff_time),
    )
    mine, back = exchange(keep, swap)
    keep, swap, x_next, i_second, g_fine, g_coarse = call(
        second_kernel, "substep",
        [VM] * 11 + [SM] + [VM] * 7,
        [SENT, SENT, FINE, FINE, FINE, FINE],
        [(3 * BP, LANES)] + WEIGHTS
        + [(4 * FP, NQ * LANES), (3 * BP, NQ * LANES), FINE, (4 * FP, NQ * LANES), FINE],
        (mine, back, x_fine, i_first, c_first, c_second, fine_star, fine_flux,
         fine_neighbors, fine_faces, fine_turns, fine_count, send_fine, send_coarse,
         stiff_time, stiff_volume, face_lift, face_project, face_rotate),
    )
    mine, back = exchange(keep, swap)
    return tuple(call(
        third_kernel, "finish",
        [VM] * 20 + [SM] + [VM] * 4,
        [(NB, NQ, LANES), (NB, NQ, 2 * LANES)],
        WEIGHTS
        + [(4 * FP, NQ * LANES), (3 * BP, NQ * LANES), FINE, (4 * FP, NQ * LANES)]
        + [(4 * FP, 2 * NQ * LANES), (3 * BP, 2 * NQ * LANES), FINE, FINE, COARSE, FINE],
        (mine, back, x_next, i_first, i_second, x_coarse, c_first, c_second, g_fine, g_coarse,
         fine_star, fine_flux, coarse_star, coarse_flux,
         fine_neighbors, fine_faces, fine_turns, coarse_neighbors, coarse_faces, coarse_turns,
         fine_count, stiff_volume, face_lift, face_project, face_rotate),
    ))


def solution(mesh):
    placed = (
        P(None, None, "dom"),
        P(None, None, "dom"),
        P(None, None, None, "dom"),
        P(None, None, None, "dom"),
        P(None, None, None, None, "dom"),
        P(None, None, None, None, "dom"),
        P(None, "dom"),
        P(None, "dom"),
        P(None, "dom"),
        P(None, "dom"),
        P(None, "dom"),
        P(None, "dom"),
        P("dom"),
        P("dom", None, None),
        P("dom", None, None),
        P(),
        P(),
        P(),
        P(),
        P(),
    )
    return jax.shard_map(
        local,
        mesh=mesh,
        in_specs=placed,
        out_specs=(P(None, None, "dom"), P(None, None, "dom")),
        check_vma=False,
    )
```

profile of v0, /device:TPU:1, one launch (start us, length us, event | category | flops | bytes accessed | tf_op | source)
XLA Modules:
  0.0 56.5 jit_solution(15656794585484751869)
XLA Ops:
  0.6 0.0 copy-start.11
  0.6 0.0 copy-start.1
  1.3 0.8 %copy.74.send_fine = s32[1,12,8]{2,1,0:T(8,128)S(1)} copy(s32[1,12,8]{1,2,0:T(8,128)} %param.33) | data formatting | bytes 768 | tf_op args[13]
  2.1 0.8 %copy.75.send_coarse = s32[1,12,4]{2,1,0:T(8,128)S(1)} copy(s32[1,12,4]{1,2,0:T(4,128)} %param.34) | data formatting | bytes 384 | tf_op args[14]
  2.9 0.9 %copy.70.fine_state = f32[20,9,128]{2,1,0:T(8,128)S(1)} copy(f32[20,9,128]{2,0,1:T(8,128)} %param.20) | data formatting | bytes 184320 | tf_op args[0]
  3.8 0.9 %copy.71.fine_star = f32[3,9,9,128]{3,2,1,0:T(8,128)S(1)} copy(f32[3,9,9,128]{3,0,2,1:T(4,128)} %param.22) | data formatting | bytes 248832 | tf_op args[2]
  4.8 1.0 %copy.72.coarse_state = f32[20,9,256]{2,1,0:T(8,128)S(1)} copy(f32[20,9,256]{2,0,1:T(8,128)} %param.21) | data formatting | bytes 368640 | tf_op args[1]
  5.8 0.0 copy-done.11
  5.8 0.1 copy.73.coarse_star
  5.9 0.0 copy-done.1
  5.9 2.5 %predict.1 = (f32[128,384]{1,0:T(8,128)S(1)}, f32[128,384]{1,0:T(8,128)S(1)}, f32[24,1152]{1,0:T(8,128)S(1)}, f32[24,1152]{1,0:T(8,128)S(1)}, f32[24,2304]{1,0:T...) custom-call(f32[20,9,128]{2,1,0:T(8,128)S(1)} %copy.70.fine_state, f32[3,9,9,128]{3,2,1,0:T(8,128)S(1)} %copy.71.fine_star, ...), custom_call_target="tpu_custom_call" | custom-call | tf_op jit(solution)/shard_map/predict/pallas_call | solution.py:386
  8.4 1.5 %collective-permute-start = (f32[128,384]{1,0:T(8,128)S(1)}, f32[128,384]{1,0:T(8,128)S(1)}, u32[]{:S(2)}, u32[]{:S(2)}) collective-permute-start(f32[128,384]{1,0:T(8,128)S(1)} %get-tuple-element.16), channel_id=1, source_target_pairs={{0,1},{1,0},{2,3},{3,2},{4,5},{5,4},{6,7},{7,6},{8,9},{9,8},{10,11... | collective-permute-start | bytes 589832 | tf_op jit(solution)/shard_map/ppermute | solution.py:411
  9.9 1.1 %collective-permute-done = f32[128,384]{1,0:T(8,128)S(1)} collective-permute-done((f32[128,384]{1,0:T(8,128)S(1)}, f32[128,384]{1,0:T(8,128)S(1)}, u32[]{:S(2)}, u32[]{:S(2)}) %collective-permute-start) | collective-permute-done | bytes 196640 | tf_op jit(solution)/shard_map/ppermute | solution.py:411
  11.0 0.0 copy-start.12
  11.0 0.0 copy-start.13
  11.0 0.0 copy-start.10
  11.1 20.1 %all_to_all.10 = f32[8,2,2,8,384]{4,3,1,2,0:T(8,128)S(1)} all-to-all(f32[8,2,2,8,384]{4,3,1,2,0:T(8,128)S(1)} %copy.76), channel_id=1, replica_groups={{0,2,4,6,8,10,12,14},{16,18,20,22,24,26,28,30},{32,34,36,38,40,42,44,46..., dimensions={0} | all-to-all | bytes 786432 | tf_op jit(solution)/shard_map/all_to_all | solution.py:413
  31.2 0.0 copy-start.5
  31.2 0.1 collective-permute-start.1
  31.3 0.0 copy-done.12
  31.4 0.0 copy-done.13
  31.4 0.1 copy.83.lift
  31.5 0.0 copy-done.10
  31.5 0.1 copy.80.fine_flux
  31.6 1.2 %collective-permute-done.1.back = f32[8,2,8,384]{3,2,1,0:T(8,128)S(1)} collective-permute-done((f32[8,2,8,384]{3,2,1,0:T(8,128)S(1)}, f32[8,2,8,384]{3,2,1,0:T(8,128)S(1)}, u32[]{:S(2)}, u32[]{:S(2)}) %collective-permute-start.1) | collective-permute-done | bytes 196640 | tf_op jit(solution)/shard_map/ppermute | solution.py:414
  32.8 0.0 copy-done
  32.8 0.0 copy-done.2
  32.8 0.0 copy-done.3
  32.8 0.0 copy-done.4
  32.8 0.0 copy-done.5
  32.8 2.7 %substep.1 = (f32[128,384]{1,0:T(8,128)S(1)}, f32[128,384]{1,0:T(8,128)S(1)}, f32[24,1152]{1,0:T(8,128)S(1)}, f32[24,1152]{1,0:T(8,128)S(1)}, f32[24,1152]{1,0:T(8,128)S(1)}, /*index=5*/f32[24,1152]{1,0:T(8,128)S(1)}) custom-call(f32[8,2,2,8,384]{4,3,2,1,0:T(8,128)S(1)} %copy.78.mine, f32[8,2,8,384]{3,2,1,0:T(8,128)S(1)} %collective-permute-done.1.back, ...), custom_call_target="tpu_custom_call" | custom-call | tf_op jit(solution)/shard_map/substep/pallas_call | solution.py:386
  35.5 0.2 collective-permute-start.2
  35.7 1.3 %collective-permute-done.2 = f32[128,384]{1,0:T(8,128)S(1)} collective-permute-done((f32[128,384]{1,0:T(8,128)S(1)}, f32[128,384]{1,0:T(8,128)S(1)}, u32[]{:S(2)}, u32[]{:S(2)}) %collective-permute-start.2) | collective-permute-done | bytes 196640 | tf_op jit(solution)/shard_map/ppermute | solution.py:411
  37.0 0.0 copy-start.9
  37.1 12.7 %all_to_all.11 = f32[8,2,2,8,384]{4,3,1,2,0:T(8,128)S(1)} all-to-all(f32[8,2,2,8,384]{4,3,1,2,0:T(8,128)S(1)} %copy.85), channel_id=1, replica_groups={{0,2,4,6,8,10,12,14},{16,18,20,22,24,26,28,30},{32,34,36,38,40,42,44,46..., dimensions={0} | all-to-all | bytes 786432 | tf_op jit(solution)/shard_map/all_to_all | solution.py:413
  49.8 0.0 copy-start.6
  49.8 0.0 copy-start.7
  49.8 0.0 copy-start.8
  49.8 0.1 collective-permute-start.3
  49.9 0.0 copy-done.9
  49.9 0.2 copy.91.coarse_flux
  50.1 1.2 %collective-permute-done.3.back = f32[8,2,8,384]{3,2,1,0:T(8,128)S(1)} collective-permute-done((f32[8,2,8,384]{3,2,1,0:T(8,128)S(1)}, f32[8,2,8,384]{3,2,1,0:T(8,128)S(1)}, u32[]{:S(2)}, u32[]{:S(2)}) %collective-permute-start.3) | collective-permute-done | bytes 196640 | tf_op jit(solution)/shard_map/ppermute | solution.py:414
  51.3 0.0 copy-done.6
  51.3 0.0 copy-done.7
  51.3 0.0 copy-done.8
  51.3 3.7 %finish.1 = (f32[20,9,128]{2,1,0:T(8,128)S(1)}, f32[20,9,256]{2,1,0:T(8,128)S(1)}) custom-call(f32[8,2,2,8,384]{4,3,2,1,0:T(8,128)S(1)} %copy.87.mine, f32[8,2,8,384]{3,2,1,0:T(8,128)S(1)} %collective-permute-done.3.back, f32[24,1152]{1,0:T(8,128)S(1)} %get-tuple-element.23.x_fine, f32[24,1152]{1,0:T(8,128)S(1)} %get-tuple-element.18.i_fine.i_first, ...), custom_call_target="tpu_custom_call" | custom-call | tf_op jit(solution)/shard_map/finish/pallas_call | solution.py:386
  55.1 0.7 %copy.94 = f32[20,9,128]{2,0,1:T(8,128)} copy(f32[20,9,128]{2,1,0:T(8,128)S(1)} %get-tuple-element.32) | data formatting | bytes 184320 | tf_op jit(solution)/shard_map/finish/pallas_call | solution.py:386
  55.7 0.8 %copy.95 = f32[20,9,256]{2,0,1:T(8,128)} copy(f32[20,9,256]{2,1,0:T(8,128)S(1)} %get-tuple-element.33) | data formatting | bytes 368640 | tf_op jit(solution)/shard_map/finish/pallas_call | solution.py:386
  (13 shorter events, 0.2 us)
Async XLA Ops:
  0.6 5.1 %copy-start.11 = (f32[3,9,9,256]{3,0,2,1:T(4,128)S(1)}, f32[3,9,9,256]{3,0,2,1:T(4,128)}, u32[]{:S(2)}) copy-start(f32[3,9,9,256]{3,0,2,1:T(4,128)} %param.23) | copy-start | bytes 746500
  0.6 5.2 %copy-start.1 = (f32[3,20,20]{2,1,0:T(8,128)S(1)}, f32[3,20,20]{2,1,0:T(8,128)}, u32[]{:S(2)}) copy-start(f32[3,20,20]{2,1,0:T(8,128)} %stiff.3) | copy-start | bytes 14404
  8.4 2.6 %collective-permute-start = (f32[128,384]{1,0:T(8,128)S(1)}, f32[128,384]{1,0:T(8,128)S(1)}, u32[]{:S(2)}, u32[]{:S(2)}) collective-permute-start(f32[128,384]{1,0:T(8,128)S(1)} %get-tuple-element.16), channel_id=1, source_target_pairs={{0,1},{1,0},{2,3},{3,2},{4,5},{5,4},{6,7},{7,6},{8,9},{9,8},{10,11... | collective-permute-start | bytes 589832 | tf_op jit(solution)/shard_map/ppermute | solution.py:411
  11.0 20.3 %copy-start.12 = (f32[4,6,20]{2,0,1:T(4,128)S(1)}, f32[4,6,20]{2,0,1:T(4,128)}, u32[]{:S(2)}) copy-start(f32[4,6,20]{2,0,1:T(4,128)} %param.38) | copy-start | bytes 5764
  11.0 20.3 %copy-start.13 = (f32[4,20,6]{1,0,2:T(4,128)S(1)}, f32[4,20,6]{1,0,2:T(4,128)}, u32[]{:S(2)}) copy-start(f32[4,20,6]{1,0,2:T(4,128)} %param.37) | copy-start | bytes 5764
  11.0 20.5 %copy-start.10 = (f32[2,4,9,9,128]{4,1,3,2,0:T(4,128)S(1)}, f32[2,4,9,9,128]{4,1,3,2,0:T(4,128)}, u32[]{:S(2)}) copy-start(f32[2,4,9,9,128]{4,1,3,2,0:T(4,128)} %param.24) | copy-start | bytes 995332
  31.2 1.6 %copy-start = (f32[3,20,20]{2,1,0:T(8,128)S(1)}, f32[3,20,20]{2,1,0:T(8,128)}, u32[]{:S(2)}) copy-start(f32[3,20,20]{2,1,0:T(8,128)} %stiff_volume.3) | copy-start | bytes 14404
  31.2 1.6 %copy-start.2 = (f32[3,6,6]{2,1,0:T(8,128)S(1)}, f32[3,6,6]{2,1,0:T(8,128)}, u32[]{:S(2)}) copy-start(f32[3,6,6]{2,1,0:T(8,128)} %rotate.3) | copy-start | bytes 1300
  31.2 1.6 %copy-start.3 = (s32[4,128]{1,0:T(4,128)S(1)}, s32[4,128]{1,0:T(4,128)}, u32[]{:S(2)}) copy-start(s32[4,128]{1,0:T(4,128)} %neighbors.3) | copy-start | bytes 6148
  31.2 1.6 %copy-start.4 = (s32[4,128]{1,0:T(4,128)S(1)}, s32[4,128]{1,0:T(4,128)}, u32[]{:S(2)}) copy-start(s32[4,128]{1,0:T(4,128)} %faces.3) | copy-start | bytes 6148
  31.2 1.6 %copy-start.5 = (s32[4,128]{1,0:T(4,128)S(1)}, s32[4,128]{1,0:T(4,128)}, u32[]{:S(2)}) copy-start(s32[4,128]{1,0:T(4,128)} %turns.3) | copy-start | bytes 6148
  31.2 1.5 %collective-permute-start.1 = (f32[8,2,8,384]{3,2,1,0:T(8,128)S(1)}, f32[8,2,8,384]{3,2,1,0:T(8,128)S(1)}, u32[]{:S(2)}, u32[]{:S(2)}) collective-permute-start(f32[8,2,8,384]{3,2,1,0:T(8,128)S(1)} %slice_bitcast_fusion.1), channel_id=1, source_target_pairs={{0,1},{1,0},{2,3},{3,2},{4,5},{5,4},{6,7},{7,6},{8,9},{9,8},{10,11... | collective-permute-start | bytes 589832 | tf_op jit(solution)/shard_map/ppermute | solution.py:414
  35.5 1.5 %collective-permute-start.2 = (f32[128,384]{1,0:T(8,128)S(1)}, f32[128,384]{1,0:T(8,128)S(1)}, u32[]{:S(2)}, u32[]{:S(2)}) collective-permute-start(f32[128,384]{1,0:T(8,128)S(1)} %get-tuple-element.22), channel_id=1, source_target_pairs={{0,1},{1,0},{2,3},{3,2},{4,5},{5,4},{6,7},{7,6},{8,9},{9,8},{10,11... | collective-permute-start | bytes 589832 | tf_op jit(solution)/shard_map/ppermute | solution.py:411
  37.0 12.9 %copy-start.9 = (f32[2,4,9,9,256]{4,1,3,2,0:T(4,128)S(1)}, f32[2,4,9,9,256]{4,1,3,2,0:T(4,128)}, u32[]{:S(2)}) copy-start(f32[2,4,9,9,256]{4,1,3,2,0:T(4,128)} %param.25) | copy-start | bytes 1990660
  49.8 1.6 %copy-start.6 = (s32[4,256]{1,0:T(4,128)S(1)}, s32[4,256]{1,0:T(4,128)}, u32[]{:S(2)}) copy-start(s32[4,256]{1,0:T(4,128)} %c_neighbors.1) | copy-start | bytes 12292
  49.8 1.6 %copy-start.7 = (s32[4,256]{1,0:T(4,128)S(1)}, s32[4,256]{1,0:T(4,128)}, u32[]{:S(2)}) copy-start(s32[4,256]{1,0:T(4,128)} %c_faces.1) | copy-start | bytes 12292
  49.8 1.5 %copy-start.8 = (s32[4,256]{1,0:T(4,128)S(1)}, s32[4,256]{1,0:T(4,128)}, u32[]{:S(2)}) copy-start(s32[4,256]{1,0:T(4,128)} %c_turns.1) | copy-start | bytes 12292
  49.8 1.5 %collective-permute-start.3 = (f32[8,2,8,384]{3,2,1,0:T(8,128)S(1)}, f32[8,2,8,384]{3,2,1,0:T(8,128)S(1)}, u32[]{:S(2)}, u32[]{:S(2)}) collective-permute-start(f32[8,2,8,384]{3,2,1,0:T(8,128)S(1)} %slice_bitcast_fusion), channel_id=1, source_target_pairs={{0,1},{1,0},{2,3},{3,2},{4,5},{5,4},{6,7},{7,6},{8,9},{9,8},{10,11... | collective-permute-start | bytes 589832 | tf_op jit(solution)/shard_map/ppermute | solution.py:414
where the time goes:
time: 56.9 us; the launch traced here: 56.5 us
  blocking collectives  32.8 us (58%)
  Pallas kernels  8.92 us (16%)
  local copies, waits for them, and re-layouts  6.53 us (11%)
  waiting for transfers between devices  4.74 us (8%)
  starting transfers between devices  1.88 us (3%)
  between operations  1.6 us (3%)
    all_to_all x2, blocking collectives, exchange(): lax.all_to_all(blocks, 'dom', 0, 0, axis_index_groups=planes(), tiled=True)  32.8 us
    pallas_call x3, Pallas kernels, call(): pl.pallas_call(kernel, name=name, in_specs=in_specs, out_specs=[VM] * len...  8.92 us
    unnamed x38, local copies, waits for them, and re-layouts  4.93 us
    ppermute x2, waiting for transfers between devices, exchange(): arrived = lax.ppermute(swap, 'dom', SIBLING)  2.38 us
    ppermute x2, waiting for transfers between devices, exchange(): back = lax.ppermute(got[:, :, 1], 'dom', SIBLING)  2.36 us
    ppermute x2, starting transfers between devices, exchange(): arrived = lax.ppermute(swap, 'dom', SIBLING)  1.71 us
    pallas_call x2, local copies, waits for them, and re-layouts, call(): pl.pallas_call(kernel, name=name, in_specs=in_specs, out_specs=[VM] * len...  1.47 us
  transfers between devices with their start and end apart: 4, of which 4 were waited for; matrix products, arithmetic and copies ran while one was open for 1% of the time, Pallas kernels for 0%

commit v1 on v0

--- a/solution.py
+++ b/solution.py
@@ -55,7 +55,7 @@
 def load_state(state_ref, x_ref, width):
     for q in range(NQ):
         x_ref[NB:BP, q * width : (q + 1) * width] = jnp.zeros((BP - NB, width), F32)
-        x_ref[0:NB, q * width : (q + 1) * width] = state_ref[:, q, :]
+        x_ref[0:NB, q * width : (q + 1) * width] = state_ref[q]
 
 
 def star_sum(t_ref, star_ref, width, tile):
@@ -65,7 +65,7 @@
         for q in range(NQ):
             t = t_ref[d * BP : (d + 1) * BP, q * width + tile * LANES : q * width + (tile + 1) * LANES]
             for p in range(NQ):
-                term = t * star_ref[d, q, p : p + 1, lanes]
+                term = t * star_ref[q, p, d : d + 1, lanes]
                 acc[p] = term if acc[p] is None else acc[p] + term
     return acc
 
@@ -118,18 +118,18 @@
     return jnp.clip(peer, 0, 2 * REACH - 1), valid
 
 
-def picker(send_ref, plane, width, slots):
+def picker(send_ref, plane, slots):
+    table = send_ref[0].astype(F32) + 1.0
+    if table.shape[0] < 8:
+        table = jnp.concatenate([table, table], axis=0)
+    lane = lax.broadcasted_iota(I32, table.shape, 1)
     rows = []
     for m in range(16):
         peer, valid = route(plane, m // 2, m % 2)
-        row = send_ref[0, pl.ds(peer, 1), :]
-        rows.append(jnp.broadcast_to(jnp.where(valid, row, -1), (8, width)))
-    big = jnp.concatenate(rows, axis=0).astype(F32)
-    s = lax.broadcasted_iota(I32, (LANES, width), 0) & (width - 1)
-    lane = lax.broadcasted_iota(I32, (LANES, width), 1)
-    index = jnp.sum(jnp.where(lane == s, big, 0.0), axis=1, keepdims=True)
+        rows.append(jnp.where(lane == jnp.where(valid, peer, -1), table, 0.0))
+    index = jnp.sum(jnp.concatenate(rows, axis=0), axis=1, keepdims=True)
     slot = lax.broadcasted_iota(I32, (LANES, slots), 1).astype(F32)
-    return jnp.where(slot == index, 1.0, 0.0).astype(BF16)
+    return jnp.where(slot + 1.0 == index, 1.0, 0.0).astype(BF16)
 
 
 def rows_of(ref, width, first, last):
@@ -144,10 +144,10 @@
 
 
 def pack(out_ref, plane, fine_ref, coarse_ref, send_fine_ref, send_coarse_ref):
-    hot = picker(send_fine_ref, plane, 8, LANES)
+    hot = picker(send_fine_ref, plane, LANES)
     out_ref[:, 0:256] = jnp.zeros((LANES, 256), F32)
     out_ref[:, 0 : NQ * BP] = picked(hot, rows_of(fine_ref, LANES, 0, NQ))
-    hot = picker(send_coarse_ref, plane, 4, 2 * LANES)
+    hot = picker(send_coarse_ref, plane, 2 * LANES)
     low = picked(hot, rows_of(coarse_ref, 2 * LANES, 0, 5))
     high = picked(hot, rows_of(coarse_ref, 2 * LANES, 5, NQ))
     high = jnp.concatenate([high, jnp.zeros((LANES, BP), F32)], axis=1)
@@ -172,14 +172,29 @@
 
 
 def first_kernel(
-    fine_state, fine_star, coarse_state, coarse_star, count, send_fine, send_coarse, stiff,
-    keep, swap, x_fine, i_fine, x_coarse, c_first, c_second,
-    w_ref, d_fine, t_fine, d_coarse, t_coarse,
+    fine_state, coarse_state, fine_star, coarse_star, send_fine, send_coarse, stiff,
+    fine_flux, coarse_flux, neighbors, faces, turns, c_neighbors, c_faces, c_turns,
+    stiff_volume, lift, project, rotate, count,
+    keep, swap, x_fine, i_fine, x_coarse, c_first, c_second, star_f, star_c, send_f, send_c,
+    flux_f, flux_c, nbr_f, face_f, turn_f, nbr_c, face_c, turn_c,
+    w_time, w_vol, w_proj, w_rot, w_lift,
+    state_f, state_c, stiff_v, vol_v, lift_v, project_v, rotate_v, lift_t,
+    d_fine, t_fine, d_coarse, t_coarse, sems,
 ):
-    fill_weight(w_ref, [stiff[d] for d in range(3)], BP, BP)
-    w = weight(w_ref, BP)
-    load_state(coarse_state, x_coarse, 2 * LANES)
-    load_state(fine_state, x_fine, LANES)
+    moves = [
+        (stiff, stiff_v), (fine_state, state_f), (fine_star, star_f), (coarse_state, state_c),
+        (coarse_star, star_c), (send_fine, send_f), (send_coarse, send_c),
+        (stiff_volume, vol_v), (lift, lift_v), (project, project_v), (rotate, rotate_v),
+        (neighbors, nbr_f), (faces, face_f), (turns, turn_f),
+        (c_neighbors, nbr_c), (c_faces, face_c), (c_turns, turn_c),
+        (fine_flux, flux_f), (coarse_flux, flux_c),
+    ]
+    copies = [pltpu.make_async_copy(s, d, sems.at[i]) for i, (s, d) in enumerate(moves)]
+    for copy in copies:
+        copy.start()
+    copies[0].wait()
+    fill_weight(w_time, [stiff_v[d] for d in range(3)], BP, BP)
+    w = weight(w_time, BP)
 
     def emit_coarse(tile, *terms):
         put(c_first, combine(FIRST_HALF, *terms), 2 * LANES, tile)
@@ -191,11 +206,32 @@
         values = combine(FIRST_HALF, *terms)
         put(i_fine, [jnp.where(live, v, 0.0) for v in values], LANES, tile)
 
-    predictor(x_coarse, d_coarse, t_coarse, coarse_star, w, 2 * LANES, emit_coarse)
-    predictor(x_fine, d_fine, t_fine, fine_star, w, LANES, emit_fine)
+    copies[1].wait()
+    load_state(state_f, x_fine, LANES)
+    copies[2].wait()
+    predictor(x_fine, d_fine, t_fine, star_f, w, LANES, emit_fine)
+    copies[3].wait()
+    load_state(state_c, x_coarse, 2 * LANES)
+    copies[4].wait()
+    predictor(x_coarse, d_coarse, t_coarse, star_c, w, 2 * LANES, emit_coarse)
+    for copy in copies[5:11]:
+        copy.wait()
+    fill_weight(w_vol, [vol_v[d] for d in range(3)], BP, BP)
+    fill_weight(w_proj, [project_v[:, f, :] for f in range(4)], FP, BP)
+    fill_weight(w_rot, [rotate_v[h] for h in range(3)], FP, FP)
+    lift_t[...] = jnp.zeros(lift_t.shape, F32)
+    for i in range(4):
+        lift_t[i * FP : i * FP + FNB, 0:NB] = lift_v[:, i, :]
+    hi, lo = halves(lift_t[...].T[0:BP, 0:32])
+    w_lift[...] = jnp.zeros(w_lift.shape, F32)
+    w_lift[:, 0:32] = hi
+    w_lift[:, 32:64] = hi
+    w_lift[:, 64:96] = lo
     core = place()[2]
-    pack(keep, core, i_fine, c_first, send_fine, send_coarse)
-    pack(swap, 1 - core, i_fine, c_first, send_fine, send_coarse)
+    pack(swap, 1 - core, i_fine, c_first, send_f, send_c)
+    pack(keep, core, i_fine, c_first, send_f, send_c)
+    for copy in copies[11:]:
+        copy.wait()
 
 
 def locate(n):
@@ -256,8 +292,8 @@
                 start = q * width + tile * LANES
                 own = p_ref[i * FP : (i + 1) * FP, start : start + LANES]
                 for p in range(NQ):
-                    term = own * flux_ref[0, i, q, p : p + 1, lanes]
-                    term = term + other * flux_ref[1, i, q, p : p + 1, lanes]
+                    term = own * flux_ref[0, q, p, i : i + 1, lanes]
+                    term = term + other * flux_ref[1, q, p, i : i + 1, lanes]
                     acc[p] = term if acc[p] is None else acc[p] + term
             for p in range(NQ):
                 l_ref[i * FP : (i + 1) * FP, p * LANES : (p + 1) * LANES] = acc[p]
@@ -270,28 +306,13 @@
         )
 
 
-def fill_corrector(stiff_volume, lift, project, rotate, w_vol, w_proj, w_rot, w_lift):
-    fill_weight(w_vol, [stiff_volume[d] for d in range(3)], BP, BP)
-    fill_weight(w_proj, [project[f] for f in range(4)], FP, BP)
-    fill_weight(w_rot, [rotate[h] for h in range(3)], FP, FP)
-    w_lift[...] = jnp.zeros(w_lift.shape, F32)
-    for i in range(4):
-        hi, lo = halves(lift[i])
-        w_lift[0:NB, i * FP : i * FP + FNB] = hi
-        w_lift[0:NB, 32 + i * FP : 32 + i * FP + FNB] = hi
-        w_lift[0:NB, 64 + i * FP : 64 + i * FP + FNB] = lo
-    return weight(w_vol, BP), weight(w_proj, BP), weight(w_rot, FP), weight(w_lift, 32)
-
-
 def second_kernel(
-    mine, back, x_fine, i_fine, c_first, c_second, fine_star, fine_flux,
-    neighbors, faces, turns, count, send_fine, send_coarse,
-    stiff, stiff_volume, lift, project, rotate,
+    mine, back, x_fine, i_fine, c_first, c_second, star_f, flux_f,
+    neighbors, faces, turns, send_fine, send_coarse, w_time, w_vol, w_proj, w_rot, w_lift, count,
     keep, swap, x_next, i_next, ghost_f, ghost_c,
-    w_ref, w_vol, w_proj, w_rot, w_lift, p_ref, t_ref, n_ref, l_ref, d_ref,
+    p_ref, t_ref, n_ref, l_ref, d_ref,
 ):
-    weights = fill_corrector(stiff_volume, lift, project, rotate, w_vol, w_proj, w_rot, w_lift)
-    fill_weight(w_ref, [stiff[d] for d in range(3)], BP, BP)
+    weights = weight(w_vol, BP), weight(w_proj, BP), weight(w_rot, FP), weight(w_lift, 32)
     unpack(mine, back, None, ghost_f, ghost_c)
     live = lax.broadcasted_iota(I32, (BP, LANES), 1) < count[0]
     tables = [
@@ -304,7 +325,7 @@
         put(x_next, [jnp.where(live, v, o) for v, o in zip(values, old)], LANES, 0)
 
     correct(
-        x_fine, i_fine, LANES, tables, neighbors, faces, turns, fine_star, fine_flux, weights,
+        x_fine, i_fine, LANES, tables, neighbors, faces, turns, star_f, flux_f, weights,
         p_ref, t_ref, n_ref, l_ref, emit_state,
     )
 
@@ -312,22 +333,21 @@
         values = combine(FIRST_HALF, *terms)
         put(i_next, [jnp.where(live, v, 0.0) for v in values], LANES, 0)
 
-    predictor(x_next, d_ref, t_ref, fine_star, weight(w_ref, BP), LANES, emit_fine)
+    predictor(x_next, d_ref, t_ref, star_f, weight(w_time, BP), LANES, emit_fine)
     core = place()[2]
+    pack(swap, 1 - core, i_next, c_second, send_fine, send_coarse)
     pack(keep, core, i_next, c_second, send_fine, send_coarse)
-    pack(swap, 1 - core, i_next, c_second, send_fine, send_coarse)
 
 
 def third_kernel(
     mine, back, x_fine, i_first, i_fine, x_coarse, c_first, c_second, g_fine, g_coarse,
     fine_star, fine_flux, coarse_star, coarse_flux,
-    neighbors, faces, turns, c_neighbors, c_faces, c_turns, count,
-    stiff_volume, lift, project, rotate,
+    neighbors, faces, turns, c_neighbors, c_faces, c_turns, w_vol, w_proj, w_rot, w_lift, count,
     fine_out, coarse_out,
-    w_vol, w_proj, w_rot, w_lift, p_ref, t_ref, n_ref, l_ref, pc_ref, tc_ref,
-    ghost_f, ghost_c, c_full, i_both,
+    p_ref, t_ref, n_ref, l_ref, pc_ref, tc_ref, ghost_f, ghost_c, c_full, i_both,
+    fine_v, coarse_v, sems,
 ):
-    weights = fill_corrector(stiff_volume, lift, project, rotate, w_vol, w_proj, w_rot, w_lift)
+    weights = weight(w_vol, BP), weight(w_proj, BP), weight(w_rot, FP), weight(w_lift, 32)
     unpack(mine, back, None, ghost_f, ghost_c)
     live = lax.broadcasted_iota(I32, (NB, LANES), 1) < count[0]
     tables = [
@@ -338,12 +358,14 @@
     def emit_fine(tile, values):
         old = get(x_fine, LANES, 0)
         for p in range(NQ):
-            fine_out[:, p, :] = jnp.where(live, values[p][:NB], old[p][:NB])
+            fine_v[p] = jnp.where(live, values[p][:NB], old[p][:NB])
 
     correct(
         x_fine, i_fine, LANES, tables, neighbors, faces, turns, fine_star, fine_flux, weights,
         p_ref, t_ref, n_ref, l_ref, emit_fine,
     )
+    fine_copy = pltpu.make_async_copy(fine_v, fine_out, sems.at[0])
+    fine_copy.start()
     c_full[...] = c_first[...] + c_second[...]
     i_both[...] = i_first[...] + i_fine[...]
     ghost_f[...] = ghost_f[...] + g_fine[...]
@@ -355,43 +377,49 @@
 
     def emit_coarse(tile, values):
         for p in range(NQ):
-            coarse_out[:, p, tile * LANES : (tile + 1) * LANES] = values[p][:NB]
+            coarse_v[p, :, tile * LANES : (tile + 1) * LANES] = values[p][:NB]
 
     correct(
         x_coarse, c_full, 2 * LANES, tables, c_neighbors, c_faces, c_turns, coarse_star,
         coarse_flux, weights, pc_ref, tc_ref, n_ref, l_ref, emit_coarse,
     )
+    coarse_copy = pltpu.make_async_copy(coarse_v, coarse_out, sems.at[1])
+    coarse_copy.start()
+    fine_copy.wait()
+    coarse_copy.wait()
 
 
 VM = pl.BlockSpec(memory_space=pltpu.VMEM)
 SM = pl.BlockSpec(memory_space=pltpu.SMEM)
-
-
-def struct(*shape):
-    return jax.ShapeDtypeStruct(shape, F32)
-
-
-def scratch(*shape):
-    return pltpu.VMEM(shape, F32)
-
+ANY = pl.BlockSpec(memory_space=pltpu.HBM)
 
 FINE = (BP, NQ * LANES)
 COARSE = (BP, 2 * NQ * LANES)
+FACES_F = (4 * FP, NQ * LANES)
+FACES_C = (4 * FP, 2 * NQ * LANES)
+STIFF_F = (3 * BP, NQ * LANES)
+STIFF_C = (3 * BP, 2 * NQ * LANES)
 SENT = (LANES, ROW)
 WEIGHTS = [(3 * BP, LANES), (4 * FP, LANES), (3 * FP, LANES), (BP, LANES)]
 PARAMS = pltpu.CompilerParams(vmem_limit_bytes=24 * 1024 * 1024)
 
 
-def call(kernel, name, in_specs, outs, scratches, args):
+def call(kernel, name, outs, scratches, args, count, hbm_in=False, hbm_out=False, sems=0, us=2):
+    if hbm_in:
+        args = [pltpu.with_memory_space_constraint(a, pltpu.HBM) for a in args]
+    kinds = [pltpu.VMEM(s, F32) if isinstance(s, tuple) else s for s in scratches]
+    if sems:
+        kinds.append(pltpu.SemaphoreType.DMA((sems,)))
     return pl.pallas_call(
         kernel,
         name=name,
-        in_specs=in_specs,
-        out_specs=[VM] * len(outs),
-        out_shape=[struct(*s) for s in outs],
-        scratch_shapes=[scratch(*s) for s in scratches],
+        in_specs=[ANY if hbm_in else VM] * len(args) + [SM] * len(count),
+        out_specs=[ANY if hbm_out else VM] * len(outs),
+        out_shape=[jax.ShapeDtypeStruct(s, F32) if isinstance(s, tuple) else s for s in outs],
+        scratch_shapes=kinds,
         compiler_params=PARAMS,
-    )(*args)
+        cost_estimate=pl.CostEstimate(flops=us * 10**9, bytes_accessed=us * 10**6, transcendentals=0),
+    )(*args, *count)
 
 
 def planes():
@@ -421,38 +449,49 @@
     fine_count, send_fine, send_coarse,
     stiff_time, stiff_volume, face_lift, face_project, face_rotate,
 ):
-    keep, swap, x_fine, i_first, x_coarse, c_first, c_second = call(
+    fine_state, coarse_state = [s.transpose(1, 0, 2) for s in (fine_state, coarse_state)]
+    fine_star, coarse_star = [s.transpose(1, 2, 0, 3) for s in (fine_star, coarse_star)]
+    fine_flux, coarse_flux = [s.transpose(0, 2, 3, 1, 4) for s in (fine_flux, coarse_flux)]
+    send_fine, send_coarse = [s.transpose(0, 2, 1) for s in (send_fine, send_coarse)]
+    face_lift = face_lift.transpose(2, 0, 1)
+    face_project = face_project.transpose(1, 0, 2)
+    count = (fine_count,)
+    links = (fine_neighbors, fine_faces, fine_turns, coarse_neighbors, coarse_faces, coarse_turns)
+    fixed = (stiff_volume, face_lift, face_project, face_rotate)
+    (keep, swap, x_fine, i_first, x_coarse, c_first, c_second, fine_star, coarse_star,
+     send_fine, send_coarse, fine_flux, coarse_flux, *rest) = call(
         first_kernel, "predict",
-        [VM, VM, VM, VM, SM, VM, VM, VM],
-        [SENT, SENT, FINE, FINE, COARSE, COARSE, COARSE],
-        [(3 * BP, LANES), FINE, (3 * BP, NQ * LANES), COARSE, (3 * BP, 2 * NQ * LANES)],
-        (fine_state, fine_star, coarse_state, coarse_star, fine_count, send_fine, send_coarse,
-         stiff_time),
-    )
+        [SENT, SENT, FINE, FINE, COARSE, COARSE, COARSE, fine_star.shape, coarse_star.shape]
+        + [jax.ShapeDtypeStruct(s.shape, I32) for s in (send_fine, send_coarse)]
+        + [fine_flux.shape, coarse_flux.shape]
+        + [jax.ShapeDtypeStruct(s.shape, I32) for s in links]
+        + WEIGHTS[:1] + WEIGHTS,
+        [fine_state.shape, coarse_state.shape, stiff_time.shape] + [f.shape for f in fixed]
+        + [(LANES, LANES), FINE, STIFF_F, COARSE, STIFF_C],
+        (fine_state, coarse_state, fine_star, coarse_star, send_fine, send_coarse, stiff_time,
+         fine_flux, coarse_flux, *links, *fixed),
+        count, hbm_in=True, sems=19,
+    )
+    links, (w_time, *weights) = rest[:6], rest[6:]
     mine, back = exchange(keep, swap)
     keep, swap, x_next, i_second, g_fine, g_coarse = call(
         second_kernel, "substep",
-        [VM] * 11 + [SM] + [VM] * 7,
         [SENT, SENT, FINE, FINE, FINE, FINE],
-        [(3 * BP, LANES)] + WEIGHTS
-        + [(4 * FP, NQ * LANES), (3 * BP, NQ * LANES), FINE, (4 * FP, NQ * LANES), FINE],
-        (mine, back, x_fine, i_first, c_first, c_second, fine_star, fine_flux,
-         fine_neighbors, fine_faces, fine_turns, fine_count, send_fine, send_coarse,
-         stiff_time, stiff_volume, face_lift, face_project, face_rotate),
+        [FACES_F, STIFF_F, FINE, FACES_F, FINE],
+        (mine, back, x_fine, i_first, c_first, c_second, fine_star, fine_flux, *links[:3],
+         send_fine, send_coarse, w_time, *weights), count,
     )
     mine, back = exchange(keep, swap)
-    return tuple(call(
+    results = call(
         third_kernel, "finish",
-        [VM] * 20 + [SM] + [VM] * 4,
-        [(NB, NQ, LANES), (NB, NQ, 2 * LANES)],
-        WEIGHTS
-        + [(4 * FP, NQ * LANES), (3 * BP, NQ * LANES), FINE, (4 * FP, NQ * LANES)]
-        + [(4 * FP, 2 * NQ * LANES), (3 * BP, 2 * NQ * LANES), FINE, FINE, COARSE, FINE],
+        [(NQ, NB, LANES), (NQ, NB, 2 * LANES)],
+        [FACES_F, STIFF_F, FINE, FACES_F, FACES_C, STIFF_C, FINE, FINE, COARSE, FINE,
+         (NQ, NB, LANES), (NQ, NB, 2 * LANES)],
         (mine, back, x_next, i_first, i_second, x_coarse, c_first, c_second, g_fine, g_coarse,
-         fine_star, fine_flux, coarse_star, coarse_flux,
-         fine_neighbors, fine_faces, fine_turns, coarse_neighbors, coarse_faces, coarse_turns,
-         fine_count, stiff_volume, face_lift, face_project, face_rotate),
-    ))
+         fine_star, fine_flux, coarse_star, coarse_flux, *links, *weights), count,
+        hbm_out=True, sems=2,
+    )
+    return tuple(r.transpose(1, 0, 2) for r in results)
 
 
 def solution(mesh):

time: 56.9 us -> 52.4 us (0.921)
  local copies, waits for them, and re-layouts: 6.53 us -> 0.14 us
  Pallas kernels: 8.92 us -> 11.1 us
    unnamed x38 -> x0, local copies, waits for them, and re-layouts: 4.93 us -> none
    pallas_call x3, Pallas kernels: 8.92 us -> 11.1 us  [call(): pl.pallas_call(kernel, name=name, in_specs=[ANY if hbm_in else VM] * len(...]
    pallas_call x2 -> x0, local copies, waits for them, and re-layouts: 1.47 us -> none  [call(): pl.pallas_call(kernel, name=name, in_specs=in_specs, out_specs=[VM] * len...]
  transfers between devices with their start and end apart: 4 -> 4, of which waited for: 4 -> 4; matrix products, arithmetic and copies ran while one was open for 1% -> 0% of each run, Pallas kernels for 0% -> 0%
where the time goes in v1:
time: 52.4 us; the launch traced here: 52.2 us
  blocking collectives  32.5 us (62%)
  Pallas kernels  11.1 us (21%)
  waiting for transfers between devices  5.16 us (10%)
  starting transfers between devices  1.89 us (4%)
  between operations  1.36 us (3%)
    all_to_all x2, blocking collectives, exchange(): lax.all_to_all(blocks, 'dom', 0, 0, axis_index_groups=planes(), tiled=True)  32.5 us
    pallas_call x3, Pallas kernels, call(): pl.pallas_call(kernel, name=name, in_specs=[ANY if hbm_in else VM] * len(...  11.1 us
    ppermute x2, waiting for transfers between devices, exchange(): back = lax.ppermute(got[:, :, 1], 'dom', SIBLING)  2.79 us
    ppermute x2, waiting for transfers between devices, exchange(): arrived = lax.ppermute(swap, 'dom', SIBLING)  2.37 us
    ppermute x2, starting transfers between devices, exchange(): arrived = lax.ppermute(swap, 'dom', SIBLING)  1.72 us
  transfers between devices with their start and end apart: 4, of which 4 were waited for; matrix products, arithmetic and copies ran while one was open for 0% of the time, Pallas kernels for 0%

profile of v1, /device:TPU:1, one launch (start us, length us, event | category | flops | bytes accessed | tf_op | source)
XLA Modules:
  0.0 52.2 jit_solution(4297697501632423822)
XLA Ops:
  1.3 4.0 %predict.1 = (f32[128,384]{1,0:T(8,128)S(1)}, f32[128,384]{1,0:T(8,128)S(1)}, f32[24,1152]{1,0:T(8,128)S(1)}, f32[24,1152]{1,0:T(8,128)S(1)}, f32[24,2304]{1,0:T...) custom-call(f32[9,20,128]{2,1,0:T(8,128)} %bitcast.33, ...), custom_call_target="tpu_custom_call" | custom-call | flops 2000000000 | bytes 2000000 | tf_op jit(solution)/shard_map/predict/pallas_call | solution.py:413
  5.3 1.5 %collective-permute-start = (f32[128,384]{1,0:T(8,128)S(1)}, f32[128,384]{1,0:T(8,128)S(1)}, u32[]{:S(2)}, u32[]{:S(2)}) collective-permute-start(f32[128,384]{1,0:T(8,128)S(1)} %get-tuple-element.35), channel_id=1, source_target_pairs={{0,1},{1,0},{2,3},{3,2},{4,5},{5,4},{6,7},{7,6},{8,9},{9,8},{10,11... | collective-permute-start | bytes 589832 | tf_op jit(solution)/shard_map/ppermute | solution.py:439
  6.8 1.1 %collective-permute-done = f32[128,384]{1,0:T(8,128)S(1)} collective-permute-done((f32[128,384]{1,0:T(8,128)S(1)}, f32[128,384]{1,0:T(8,128)S(1)}, u32[]{:S(2)}, u32[]{:S(2)}) %collective-permute-start) | collective-permute-done | bytes 196640 | tf_op jit(solution)/shard_map/ppermute | solution.py:439
  7.9 20.0 %all_to_all.10 = f32[8,2,2,8,384]{4,3,1,2,0:T(8,128)S(1)} all-to-all(f32[8,2,2,8,384]{4,3,1,2,0:T(8,128)S(1)} %copy.30), channel_id=1, replica_groups={{0,2,4,6,8,10,12,14},{16,18,20,22,24,26,28,30},{32,34,36,38,40,42,44,46..., dimensions={0} | all-to-all | bytes 786432 | tf_op jit(solution)/shard_map/all_to_all | solution.py:441
  27.9 0.1 collective-permute-start.1
  28.1 1.4 %collective-permute-done.1.back = f32[8,2,8,384]{3,2,1,0:T(8,128)S(1)} collective-permute-done((f32[8,2,8,384]{3,2,1,0:T(8,128)S(1)}, f32[8,2,8,384]{3,2,1,0:T(8,128)S(1)}, u32[]{:S(2)}, u32[]{:S(2)}) %collective-permute-start.1) | collective-permute-done | bytes 196640 | tf_op jit(solution)/shard_map/ppermute | solution.py:442
  29.5 2.6 %substep.1 = (f32[128,384]{1,0:T(8,128)S(1)}, f32[128,384]{1,0:T(8,128)S(1)}, f32[24,1152]{1,0:T(8,128)S(1)}, f32[24,1152]{1,0:T(8,128)S(1)}, f32[24,1152]{1,0:T(8,128)S(1)}, /*index=5*/f32[24,1152]{1,0:T(8,128)S(1)}) custom-call(f32[8,2,2,8,384]{4,3,2,1,0:T(8,128)S(1)} %copy.32.mine, f32[8,2,8,384]{3,2,1,0:T(8,128)S(1)} %collective-permute-done.1.back, ...), custom_call_target="tpu_custom_call" | custom-call | flops 2000000000 | bytes 2000000 | tf_op jit(solution)/shard_map/substep/pallas_call | solution.py:413
  32.0 0.2 collective-permute-start.2
  32.3 1.3 %collective-permute-done.2 = f32[128,384]{1,0:T(8,128)S(1)} collective-permute-done((f32[128,384]{1,0:T(8,128)S(1)}, f32[128,384]{1,0:T(8,128)S(1)}, u32[]{:S(2)}, u32[]{:S(2)}) %collective-permute-start.2) | collective-permute-done | bytes 196640 | tf_op jit(solution)/shard_map/ppermute | solution.py:439
  33.6 12.6 %all_to_all.11 = f32[8,2,2,8,384]{4,3,1,2,0:T(8,128)S(1)} all-to-all(f32[8,2,2,8,384]{4,3,1,2,0:T(8,128)S(1)} %copy.33), channel_id=1, replica_groups={{0,2,4,6,8,10,12,14},{16,18,20,22,24,26,28,30},{32,34,36,38,40,42,44,46..., dimensions={0} | all-to-all | bytes 786432 | tf_op jit(solution)/shard_map/all_to_all | solution.py:441
  46.2 0.1 collective-permute-start.3
  46.3 1.4 %collective-permute-done.3.back = f32[8,2,8,384]{3,2,1,0:T(8,128)S(1)} collective-permute-done((f32[8,2,8,384]{3,2,1,0:T(8,128)S(1)}, f32[8,2,8,384]{3,2,1,0:T(8,128)S(1)}, u32[]{:S(2)}, u32[]{:S(2)}) %collective-permute-start.3) | collective-permute-done | bytes 196640 | tf_op jit(solution)/shard_map/ppermute | solution.py:442
  47.7 4.5 %finish.1 = (f32[9,20,128]{2,1,0:T(8,128)}, f32[9,20,256]{2,1,0:T(8,128)}) custom-call(f32[8,2,2,8,384]{4,3,2,1,0:T(8,128)S(1)} %copy.35.mine, f32[8,2,8,384]{3,2,1,0:T(8,128)S(1)} %collective-permute-done.3.back, f32[24,1152]{1,0:T(8,128)S(1)} %get-tuple-element.54.x_fine, f32[24,1152]{1,0:T(8,128)S(1)} %get-tuple-element.37.i_fine.i_first, ...), custom_call_target="tpu_custom_call" | custom-call | flops 2000000000 | bytes 2000000 | tf_op jit(solution)/shard_map/finish/pallas_call | solution.py:413
  (8 shorter events, 0.2 us)
Async XLA Ops:
  5.3 2.6 %collective-permute-start = (f32[128,384]{1,0:T(8,128)S(1)}, f32[128,384]{1,0:T(8,128)S(1)}, u32[]{:S(2)}, u32[]{:S(2)}) collective-permute-start(f32[128,384]{1,0:T(8,128)S(1)} %get-tuple-element.35), channel_id=1, source_target_pairs={{0,1},{1,0},{2,3},{3,2},{4,5},{5,4},{6,7},{7,6},{8,9},{9,8},{10,11... | collective-permute-start | bytes 589832 | tf_op jit(solution)/shard_map/ppermute | solution.py:439
  27.9 1.5 %collective-permute-start.1 = (f32[8,2,8,384]{3,2,1,0:T(8,128)S(1)}, f32[8,2,8,384]{3,2,1,0:T(8,128)S(1)}, u32[]{:S(2)}, u32[]{:S(2)}) collective-permute-start(f32[8,2,8,384]{3,2,1,0:T(8,128)S(1)} %slice_bitcast_fusion.1), channel_id=1, source_target_pairs={{0,1},{1,0},{2,3},{3,2},{4,5},{5,4},{6,7},{7,6},{8,9},{9,8},{10,11... | collective-permute-start | bytes 589832 | tf_op jit(solution)/shard_map/ppermute | solution.py:442
  32.0 1.5 %collective-permute-start.2 = (f32[128,384]{1,0:T(8,128)S(1)}, f32[128,384]{1,0:T(8,128)S(1)}, u32[]{:S(2)}, u32[]{:S(2)}) collective-permute-start(f32[128,384]{1,0:T(8,128)S(1)} %get-tuple-element.53), channel_id=1, source_target_pairs={{0,1},{1,0},{2,3},{3,2},{4,5},{5,4},{6,7},{7,6},{8,9},{9,8},{10,11... | collective-permute-start | bytes 589832 | tf_op jit(solution)/shard_map/ppermute | solution.py:439
  46.2 1.5 %collective-permute-start.3 = (f32[8,2,8,384]{3,2,1,0:T(8,128)S(1)}, f32[8,2,8,384]{3,2,1,0:T(8,128)S(1)}, u32[]{:S(2)}, u32[]{:S(2)}) collective-permute-start(f32[8,2,8,384]{3,2,1,0:T(8,128)S(1)} %slice_bitcast_fusion), channel_id=1, source_target_pairs={{0,1},{1,0},{2,3},{3,2},{4,5},{5,4},{6,7},{7,6},{8,9},{9,8},{10,11... | collective-permute-start | bytes 589832 | tf_op jit(solution)/shard_map/ppermute | solution.py:442

commit v2 on v1

v2 whole, which is shorter than its diff:
```python
from functools import partial

import jax
import jax.numpy as jnp
from jax import lax
from jax.experimental import pallas as pl
from jax.experimental.pallas import tpu as pltpu
from jax.sharding import PartitionSpec as P

NB = 20
NQ = 9
FNB = 6
REACH = 6
BP = 24
FP = 8
LANES = 128
ROW = 384
FIRST_HALF = (0.5, 0.125, 1.0 / 48.0)
SECOND_HALF = (0.5, 0.375, 7.0 / 48.0)
F32 = jnp.float32
BF16 = jnp.bfloat16
I32 = jnp.int32
N_DEV = 128
BLOCKS = 13
KEPT = 48


def halves(x):
    hi = x.astype(BF16).astype(F32)
    return hi, x - hi


def stacked(x):
    hi, lo = halves(x)
    return jnp.concatenate([hi, lo, hi], axis=0).astype(BF16)


def fill_weight(ref, blocks, row_step, col_step):
    ref[...] = jnp.zeros(ref.shape, F32)
    for i, block in enumerate(blocks):
        rows, cols = block.shape
        hi, lo = halves(block)
        span = slice(i * row_step, i * row_step + rows)
        ref[span, 0:cols] = hi
        ref[span, col_step : col_step + cols] = hi
        ref[span, 2 * col_step : 2 * col_step + cols] = lo


def weight(ref, depth):
    return ref[:, 0 : 3 * depth].astype(BF16)


def mm(w, x):
    return jnp.dot(w, stacked(x), preferred_element_type=F32)


def load_state(state_ref, x_ref, width):
    for q in range(NQ):
        x_ref[NB:BP, q * width : (q + 1) * width] = jnp.zeros((BP - NB, width), F32)
        x_ref[0:NB, q * width : (q + 1) * width] = state_ref[q]


def star_sum(t_ref, star_ref, width, tile):
    lanes = slice(tile * LANES, (tile + 1) * LANES)
    acc = [None] * NQ
    for q in range(NQ):
        for d in range(3):
            t = t_ref[d * BP : (d + 1) * BP, q * width + tile * LANES : q * width + (tile + 1) * LANES]
            for p in range(NQ):
                term = t * star_ref[q, p, d : d + 1, lanes]
                acc[p] = term if acc[p] is None else acc[p] + term
    return acc


def put(ref, values, width, tile):
    for p in range(NQ):
        ref[:, p * width + tile * LANES : p * width + (tile + 1) * LANES] = values[p]


def get(ref, width, tile):
    return [
        ref[:, p * width + tile * LANES : p * width + (tile + 1) * LANES] for p in range(NQ)
    ]


def first_term(x_ref, d_ref, t_ref, star_ref, width):
    for tile in range(width // LANES):
        put(d_ref, star_sum(t_ref, star_ref, width, tile), width, tile)


def second_term(x_ref, d_ref, t_ref, star_ref, width, emit):
    for tile in range(width // LANES):
        second = star_sum(t_ref, star_ref, width, tile)
        emit(tile, get(x_ref, width, tile), get(d_ref, width, tile), second)


def combine(weights, state, neg_first, second):
    return [
        weights[0] * s - weights[1] * f + weights[2] * g
        for s, f, g in zip(state, neg_first, second)
    ]


def place():
    me = lax.axis_index("dom").astype(I32)
    return me, me >> 1, me & 1


def route(block):
    me, chip, core = place()
    if block == 12:
        offset = 1 - 2 * core
    else:
        sender = core if block < 6 else 1 - core
        ahead = 1 - 2 * sender
        distance = (block % 6) // 2 + 1
        offset = 2 * ahead * distance + (sender ^ (block % 2)) - core
    target = me + offset
    valid = (target >= 0) & (target < N_DEV) & (offset >= -REACH) & (offset <= REACH)
    peer = jnp.where(offset < 0, offset + REACH, offset + REACH - 1)
    return jnp.where(valid, peer, -1)


def picker(send_ref, slots):
    table = send_ref[0].astype(F32) + 1.0
    if table.shape[0] < 8:
        table = jnp.concatenate([table, table], axis=0)
    lane = lax.broadcasted_iota(I32, table.shape, 1)
    rows = []
    for block in range(BLOCKS):
        rows.append(jnp.where(lane == route(block), table, 0.0))
    index = jnp.sum(jnp.concatenate(rows, axis=0), axis=1, keepdims=True)
    slot = lax.broadcasted_iota(I32, (BLOCKS * 8, slots), 1).astype(F32)
    return jnp.where(slot + 1.0 == index, 1.0, 0.0).astype(BF16)


def rows_of(ref, width, first, last):
    return jnp.concatenate([ref[:, q * width : (q + 1) * width] for q in range(first, last)], axis=0)


def picked(hot, field):
    hi, lo = halves(field)
    both = jnp.concatenate([hi, lo], axis=1).astype(BF16)
    hots = jnp.concatenate([hot, hot], axis=1)
    return lax.dot_general(hots, both, (((1,), (1,)), ((), ())), preferred_element_type=F32)


def pack(keep_ref, swap_ref, fine_ref, coarse_ref, send_fine_ref, send_coarse_ref):
    fine = picked(picker(send_fine_ref, LANES), rows_of(fine_ref, LANES, 0, NQ))
    hot = picker(send_coarse_ref, 2 * LANES)
    low = picked(hot, rows_of(coarse_ref, 2 * LANES, 0, 5))
    high = picked(hot, rows_of(coarse_ref, 2 * LANES, 5, NQ))
    high = jnp.concatenate([high, jnp.zeros((BLOCKS * 8, BP), F32)], axis=1)
    s = lax.broadcasted_iota(I32, (BLOCKS * 8, 5 * BP), 0) & 7
    coarse = jnp.where(s < 4, low, high)
    for ref, rows in ((keep_ref, slice(0, KEPT)), (swap_ref, slice(KEPT, BLOCKS * 8))):
        ref[:, 128:ROW] = jnp.zeros((ref.shape[0], ROW - LANES), F32)
        ref[:, 0 : NQ * BP] = fine[rows]
        ref[:, 256 : 256 + 5 * BP] = coarse[rows]


def unpack(arrived, fine_ref, coarse_ref):
    *direct, back, sibling = arrived
    parts = []
    for ref in direct:
        parts += [ref[0:8], ref[16:24]]
    parts += [back[...], sibling[KEPT : KEPT + 8], jnp.zeros((LANES - BLOCKS * 8, ROW), F32)]
    rows = jnp.concatenate(parts, axis=0)
    turned = [rows[:, t * LANES : (t + 1) * LANES].T for t in range(3)]
    fine = jnp.concatenate(turned[:2], axis=0)
    for q in range(NQ):
        fine_ref[:, q * LANES : (q + 1) * LANES] = fine[q * BP : (q + 1) * BP]
    for q in range(5):
        coarse_ref[:, q * LANES : (q + 1) * LANES] = turned[2][q * BP : (q + 1) * BP]


def first_kernel(
    fine_state, coarse_state, fine_star, coarse_star, send_fine, send_coarse, stiff,
    fine_flux, coarse_flux, neighbors, faces, turns, c_neighbors, c_faces, c_turns,
    stiff_volume, lift, project, rotate, count,
    keep, swap, x_fine, i_fine, x_coarse, c_first, c_second, star_f, star_c, send_f, send_c,
    flux_f, flux_c, nbr_f, face_f, turn_f, nbr_c, face_c, turn_c,
    w_time, w_vol, w_proj, w_rot, w_lift,
    state_f, state_c, stiff_v, vol_v, lift_v, project_v, rotate_v, lift_t,
    d_fine, t_fine, d_coarse, t_coarse, sems,
):
    moves = [
        (stiff, stiff_v), (fine_state, state_f), (fine_star, star_f), (coarse_state, state_c),
        (coarse_star, star_c), (send_fine, send_f), (send_coarse, send_c),
        (stiff_volume, vol_v), (lift, lift_v), (project, project_v), (rotate, rotate_v),
        (neighbors, nbr_f), (faces, face_f), (turns, turn_f),
        (c_neighbors, nbr_c), (c_faces, face_c), (c_turns, turn_c),
        (fine_flux, flux_f), (coarse_flux, flux_c),
    ]
    copies = [pltpu.make_async_copy(s, d, sems.at[i]) for i, (s, d) in enumerate(moves)]
    for copy in copies:
        copy.start()
    copies[0].wait()
    fill_weight(w_time, [stiff_v[d] for d in range(3)], BP, BP)
    w = weight(w_time, BP)

    def emit_coarse(tile, *terms):
        put(c_first, combine(FIRST_HALF, *terms), 2 * LANES, tile)
        put(c_second, combine(SECOND_HALF, *terms), 2 * LANES, tile)

    live = lax.broadcasted_iota(I32, (BP, LANES), 1) < count[0]

    def emit_fine(tile, *terms):
        values = combine(FIRST_HALF, *terms)
        put(i_fine, [jnp.where(live, v, 0.0) for v in values], LANES, tile)

    copies[1].wait()
    load_state(state_f, x_fine, LANES)
    t_fine[...] = mm(w, x_fine[...])
    copies[3].wait()
    load_state(state_c, x_coarse, 2 * LANES)
    t_coarse[...] = mm(w, x_coarse[...])
    copies[2].wait()
    first_term(x_fine, d_fine, t_fine, star_f, LANES)
    t_fine[...] = mm(w, d_fine[...])
    copies[4].wait()
    first_term(x_coarse, d_coarse, t_coarse, star_c, 2 * LANES)
    t_coarse[...] = mm(w, d_coarse[...])
    second_term(x_fine, d_fine, t_fine, star_f, LANES, emit_fine)
    second_term(x_coarse, d_coarse, t_coarse, star_c, 2 * LANES, emit_coarse)
    for copy in copies[5:11]:
        copy.wait()
    fill_weight(w_vol, [vol_v[d] for d in range(3)], BP, BP)
    fill_weight(w_proj, [project_v[:, f, :] for f in range(4)], FP, BP)
    w_rot[...] = jnp.zeros(w_rot.shape, F32)
    for h in range(3):
        w_rot[h * FP : h * FP + FNB, 0:FNB] = rotate_v[h]
    lift_t[...] = jnp.zeros(lift_t.shape, F32)
    for i in range(4):
        lift_t[i * FP : i * FP + FNB, 0:NB] = lift_v[:, i, :]
    hi, lo = halves(lift_t[...].T[0:BP, 0:32])
    w_lift[...] = jnp.zeros(w_lift.shape, F32)
    w_lift[:, 0:32] = hi
    w_lift[:, 32:64] = hi
    w_lift[:, 64:96] = lo
    pack(keep, swap, i_fine, c_first, send_f, send_c)
    for copy in copies[11:]:
        copy.wait()


def locate(n):
    me, chip, core = place()
    local = n < 384
    fine = n < 480
    g = jnp.where(fine, n - 384, n - 480)
    j = jnp.where(fine, g >> 3, g >> 2)
    s = jnp.where(fine, g & 7, g & 3)
    offset = j - REACH + jnp.where(j >= REACH, 1, 0)
    source = me - offset
    away = (source >> 1) - chip
    apart = jnp.abs(away)
    ahead = 1 - 2 * core
    direct = away * ahead < 0
    other = (source & 1) ^ core
    block = 2 * (apart - 1) + jnp.where(direct, other, 7 - other)
    block = jnp.where(away == 0, 12, block)
    lane = jnp.where(local, n & 127, block * 8 + s)
    tile = jnp.where(local, n >> 7, jnp.where(fine, 3, 4))
    return tile, lane


def spread(row_ref, i, tile):
    return jnp.broadcast_to(row_ref[i : i + 1, tile * LANES : (tile + 1) * LANES], (8, LANES))


def pick(options, bits):
    if len(options) == 1:
        return options[0]
    pairs = [options[i : i + 2] for i in range(0, len(options), 2)]
    merged = [jnp.where(bits[0], p[1], p[0]) if len(p) == 2 else p[0] for p in pairs]
    return pick(merged, bits[1:])


def bits_of(number, count):
    return [(number & (1 << k)) != 0 for k in range(count)]


def correct(
    state_ref, width, own_ref, tables, neighbors, faces, turns, star_ref, flux_ref, w_rot, w_lift,
    t_ref, n_ref, l_ref, emit,
):
    turned = [
        [jnp.broadcast_to(w_rot[h * FP : (h + 1) * FP, b : b + 1], (FP, LANES)) for h in range(3)]
        for b in range(FNB)
    ]
    for tile in range(width // LANES):
        lanes = slice(tile * LANES, (tile + 1) * LANES)
        for i in range(4):
            kind, lane = locate(spread(neighbors, i, tile))
            later = jnp.where(kind == 4, lane + 4, lane)
            face = spread(faces, i, tile)
            turn = spread(turns, i, tile)
            kinds = bits_of(kind, 3)
            numbers = bits_of(face, 2)
            for q in range(NQ):
                at = lane if q < 5 else later
                found = []
                for k, (ref, ref_width, ref_tile) in enumerate(tables):
                    start = (q if k < 4 else q % 5) * ref_width + ref_tile * LANES
                    found.append(pick([
                        jnp.take_along_axis(
                            ref[f * FP : (f + 1) * FP, start : start + LANES], at, axis=1
                        )
                        for f in range(4)
                    ], numbers))
                n_ref[i, :, q * LANES : (q + 1) * LANES] = pick(found, kinds)
            turn_by = [pick(turned[b], bits_of(turn, 2)) for b in range(FNB)]
            acc = [None] * NQ
            for q in range(NQ):
                at = slice(q * LANES, (q + 1) * LANES)
                other = turn_by[0] * n_ref[i, 0:1, at]
                for b in range(1, FNB):
                    other = other + turn_by[b] * n_ref[i, b : b + 1, at]
                start = q * width + tile * LANES
                own = own_ref[i * FP : (i + 1) * FP, start : start + LANES]
                for p in range(NQ):
                    term = own * flux_ref[0, q, p, i : i + 1, lanes]
                    term = term + other * flux_ref[1, q, p, i : i + 1, lanes]
                    acc[p] = term if acc[p] is None else acc[p] + term
            for p in range(NQ):
                l_ref[i * FP : (i + 1) * FP, p * LANES : (p + 1) * LANES] = acc[p]
        lifted = mm(w_lift, l_ref[...])
        volume = star_sum(t_ref, star_ref, width, tile)
        state = get(state_ref, width, tile)
        emit(
            tile,
            [state[p] + (volume[p] + lifted[:, p * LANES : (p + 1) * LANES]) for p in range(NQ)],
        )


def second_kernel(
    got_1, got_2, got_3, back, sibling, x_fine, i_fine, c_first, c_second, star_f, flux_f,
    neighbors, faces, turns, send_fine, send_coarse, w_time, w_vol, w_proj, w_rot, w_lift, count,
    keep, swap, x_next, i_next, p_own, p_coarse, p_gf, p_gc,
    ghost_f, ghost_c, t_ref, n_ref, l_ref, d_ref,
):
    w_v, w_p = weight(w_vol, BP), weight(w_proj, BP)
    t_ref[...] = mm(w_v, i_fine[...])
    p_own[...] = mm(w_p, i_fine[...])
    p_coarse[...] = mm(w_p, c_first[...])
    unpack((got_1, got_2, got_3, back, sibling), ghost_f, ghost_c)
    p_gf[...] = mm(w_p, ghost_f[...])
    p_gc[...] = mm(w_p, ghost_c[...])
    live = lax.broadcasted_iota(I32, (BP, LANES), 1) < count[0]
    tables = [
        (p_own, LANES, 0), (p_coarse, 2 * LANES, 0), (p_coarse, 2 * LANES, 1),
        (p_gf, LANES, 0), (p_gc, LANES, 0),
    ]

    def emit_state(tile, values):
        old = get(x_fine, LANES, 0)
        put(x_next, [jnp.where(live, v, o) for v, o in zip(values, old)], LANES, 0)

    correct(
        x_fine, LANES, p_own, tables, neighbors, faces, turns, star_f, flux_f,
        w_rot, weight(w_lift, 32), t_ref, n_ref, l_ref, emit_state,
    )

    def emit_fine(tile, *terms):
        values = combine(FIRST_HALF, *terms)
        put(i_next, [jnp.where(live, v, 0.0) for v in values], LANES, 0)

    w = weight(w_time, BP)
    t_ref[...] = mm(w, x_next[...])
    first_term(x_next, d_ref, t_ref, star_f, LANES)
    t_ref[...] = mm(w, d_ref[...])
    second_term(x_next, d_ref, t_ref, star_f, LANES, emit_fine)
    pack(keep, swap, i_next, c_second, send_fine, send_coarse)


def third_kernel(
    got_1, got_2, got_3, back, sibling, x_fine, i_fine, x_coarse, c_first, c_second, p_own, p_coarse, p_gf, p_gc,
    fine_star, fine_flux, coarse_star, coarse_flux,
    neighbors, faces, turns, c_neighbors, c_faces, c_turns, w_vol, w_proj, w_rot, w_lift, count,
    fine_out, coarse_out,
    q_own, q_coarse, q_gf, q_gc, ghost_f, ghost_c, t_ref, tc_ref, n_ref, l_ref,
    fine_v, coarse_v, sems,
):
    w_v, w_p, w_l = weight(w_vol, BP), weight(w_proj, BP), weight(w_lift, 32)
    t_ref[...] = mm(w_v, i_fine[...])
    q_own[...] = mm(w_p, i_fine[...])
    q_coarse[...] = mm(w_p, c_second[...])
    tc_ref[...] = mm(w_v, c_first[...] + c_second[...])
    unpack((got_1, got_2, got_3, back, sibling), ghost_f, ghost_c)
    q_gf[...] = mm(w_p, ghost_f[...])
    q_gc[...] = mm(w_p, ghost_c[...])
    live = lax.broadcasted_iota(I32, (NB, LANES), 1) < count[0]
    tables = [
        (q_own, LANES, 0), (q_coarse, 2 * LANES, 0), (q_coarse, 2 * LANES, 1),
        (q_gf, LANES, 0), (q_gc, LANES, 0),
    ]

    def emit_fine(tile, values):
        old = get(x_fine, LANES, 0)
        for p in range(NQ):
            fine_v[p] = jnp.where(live, values[p][:NB], old[p][:NB])

    correct(
        x_fine, LANES, q_own, tables, neighbors, faces, turns, fine_star, fine_flux,
        w_rot, w_l, t_ref, n_ref, l_ref, emit_fine,
    )
    fine_copy = pltpu.make_async_copy(fine_v, fine_out, sems.at[0])
    fine_copy.start()
    for total, prior in ((q_own, p_own), (q_coarse, p_coarse), (q_gf, p_gf), (q_gc, p_gc)):
        total[...] = total[...] + prior[...]

    def emit_coarse(tile, values):
        for p in range(NQ):
            coarse_v[p, :, tile * LANES : (tile + 1) * LANES] = values[p][:NB]

    correct(
        x_coarse, 2 * LANES, q_coarse, tables, c_neighbors, c_faces, c_turns, coarse_star,
        coarse_flux, w_rot, w_l, tc_ref, n_ref, l_ref, emit_coarse,
    )
    coarse_copy = pltpu.make_async_copy(coarse_v, coarse_out, sems.at[1])
    coarse_copy.start()
    fine_copy.wait()
    coarse_copy.wait()


VM = pl.BlockSpec(memory_space=pltpu.VMEM)
SM = pl.BlockSpec(memory_space=pltpu.SMEM)
ANY = pl.BlockSpec(memory_space=pltpu.HBM)

FINE = (BP, NQ * LANES)
COARSE = (BP, 2 * NQ * LANES)
FACES_F = (4 * FP, NQ * LANES)
FACES_C = (4 * FP, 2 * NQ * LANES)
STIFF_F = (3 * BP, NQ * LANES)
STIFF_C = (3 * BP, 2 * NQ * LANES)
GHOST_C = (BP, 5 * LANES)
FACES_G = (4 * FP, 5 * LANES)
PICKED = (4, FP, NQ * LANES)
WEIGHTS = [(3 * BP, LANES), (4 * FP, LANES), (3 * FP, LANES), (BP, LANES)]
PARAMS = pltpu.CompilerParams(vmem_limit_bytes=24 * 1024 * 1024)


def call(kernel, name, outs, scratches, args, count, hbm_in=False, hbm_out=False, sems=0, us=2):
    if hbm_in:
        args = [pltpu.with_memory_space_constraint(a, pltpu.HBM) for a in args]
    kinds = [pltpu.VMEM(s, F32) if isinstance(s, tuple) else s for s in scratches]
    if sems:
        kinds.append(pltpu.SemaphoreType.DMA((sems,)))
    return pl.pallas_call(
        kernel,
        name=name,
        in_specs=[ANY if hbm_in else VM] * len(args) + [SM] * len(count),
        out_specs=[ANY if hbm_out else VM] * len(outs),
        out_shape=[jax.ShapeDtypeStruct(s, F32) if isinstance(s, tuple) else s for s in outs],
        scratch_shapes=kinds,
        compiler_params=PARAMS,
        cost_estimate=pl.CostEstimate(flops=us * 10**9, bytes_accessed=us * 10**6, transcendentals=0),
    )(*args, *count)


SIBLING = [(i, i ^ 1) for i in range(N_DEV)]


def ahead_by(distance):
    step = 2 * distance
    return [(i, (i + (step if i % 2 == 0 else -step)) % N_DEV) for i in range(N_DEV)]


def exchange(keep, swap):
    sibling = lax.ppermute(swap, "dom", SIBLING)
    sent = [jnp.concatenate([keep[16 * d : 16 * d + 16], sibling[16 * d : 16 * d + 16]]) for d in range(3)]
    got = [None] * 3
    for d in (2, 1, 0):
        got[d] = lax.ppermute(sent[d], "dom", ahead_by(d + 1))
    rest = [g.reshape(2, 2, 8, ROW)[:, 1].reshape(16, ROW) for g in got]
    back = lax.ppermute(jnp.concatenate(rest), "dom", SIBLING)
    return *got, back, sibling


def local(
    fine_state, coarse_state, fine_star, coarse_star, fine_flux, coarse_flux,
    fine_neighbors, fine_faces, fine_turns, coarse_neighbors, coarse_faces, coarse_turns,
    fine_count, send_fine, send_coarse,
    stiff_time, stiff_volume, face_lift, face_project, face_rotate,
):
    fine_state, coarse_state = [s.transpose(1, 0, 2) for s in (fine_state, coarse_state)]
    fine_star, coarse_star = [s.transpose(1, 2, 0, 3) for s in (fine_star, coarse_star)]
    fine_flux, coarse_flux = [s.transpose(0, 2, 3, 1, 4) for s in (fine_flux, coarse_flux)]
    send_fine, send_coarse = [s.transpose(0, 2, 1) for s in (send_fine, send_coarse)]
    face_lift = face_lift.transpose(2, 0, 1)
    face_project = face_project.transpose(1, 0, 2)
    count = (fine_count,)
    links = (fine_neighbors, fine_faces, fine_turns, coarse_neighbors, coarse_faces, coarse_turns)
    fixed = (stiff_volume, face_lift, face_project, face_rotate)
    (keep, swap, x_fine, i_first, x_coarse, c_first, c_second, fine_star, coarse_star,
     send_fine, send_coarse, fine_flux, coarse_flux, *rest) = call(
        first_kernel, "predict",
        [(KEPT, ROW), (KEPT + 8, ROW), FINE, FINE, COARSE, COARSE, COARSE, fine_star.shape, coarse_star.shape]
        + [jax.ShapeDtypeStruct(s.shape, I32) for s in (send_fine, send_coarse)]
        + [fine_flux.shape, coarse_flux.shape]
        + [jax.ShapeDtypeStruct(s.shape, I32) for s in links]
        + WEIGHTS[:1] + WEIGHTS,
        [fine_state.shape, coarse_state.shape, stiff_time.shape] + [f.shape for f in fixed]
        + [(LANES, LANES), FINE, STIFF_F, COARSE, STIFF_C],
        (fine_state, coarse_state, fine_star, coarse_star, send_fine, send_coarse, stiff_time,
         fine_flux, coarse_flux, *links, *fixed),
        count, hbm_in=True, sems=19,
    )
    links, (w_time, *weights) = rest[:6], rest[6:]
    arrived = exchange(keep, swap)
    keep, swap, x_next, i_second, *tables = call(
        second_kernel, "substep",
        [(KEPT, ROW), (KEPT + 8, ROW), FINE, FINE, FACES_F, FACES_C, FACES_F, FACES_G],
        [FINE, GHOST_C, STIFF_F, PICKED, FACES_F, FINE],
        (*arrived, x_fine, i_first, c_first, c_second, fine_star, fine_flux, *links[:3],
         send_fine, send_coarse, w_time, *weights), count,
    )
    arrived = exchange(keep, swap)
    results = call(
        third_kernel, "finish",
        [(NQ, NB, LANES), (NQ, NB, 2 * LANES)],
        [FACES_F, FACES_C, FACES_F, FACES_G, FINE, GHOST_C, STIFF_F, STIFF_C, PICKED, FACES_F,
         (NQ, NB, LANES), (NQ, NB, 2 * LANES)],
        (*arrived, x_next, i_second, x_coarse, c_first, c_second, *tables,
         fine_star, fine_flux, coarse_star, coarse_flux, *links, *weights), count,
        hbm_out=True, sems=2,
    )
    return tuple(r.transpose(1, 0, 2) for r in results)


def solution(mesh):
    placed = (
        P(None, None, "dom"),
        P(None, None, "dom"),
        P(None, None, None, "dom"),
        P(None, None, None, "dom"),
        P(None, None, None, None, "dom"),
        P(None, None, None, None, "dom"),
        P(None, "dom"),
        P(None, "dom"),
        P(None, "dom"),
        P(None, "dom"),
        P(None, "dom"),
        P(None, "dom"),
        P("dom"),
        P("dom", None, None),
        P("dom", None, None),
        P(),
        P(),
        P(),
        P(),
        P(),
    )
    return jax.shard_map(
        local,
        mesh=mesh,
        in_specs=placed,
        out_specs=(P(None, None, "dom"), P(None, None, "dom")),
        check_vma=False,
    )
```

time: 52.4 us -> 43.2 us (0.82)
  blocking collectives: 32.5 us -> 0 us
  starting transfers between devices: 1.89 us -> 18.5 us
  waiting for transfers between devices: 5.16 us -> 12.4 us
    all_to_all x2 -> x0, blocking collectives: 32.5 us -> none  [exchange(): lax.all_to_all(blocks, 'dom', 0, 0, axis_index_groups=planes(), tiled=True)]
    ppermute x4 -> x10, starting transfers between devices: 1.89 us -> 18.5 us  [the longest x6 15.4 us: exchange(): got[d] = lax.ppermute(sent[d], 'dom', ahead_by(d + 1))]
    ppermute x4 -> x10, waiting for transfers between devices: 5.16 us -> 12.4 us  [the longest x6 8.23 us: exchange(): got[d] = lax.ppermute(sent[d], 'dom', ahead_by(d + 1))]
  transfers between devices with their start and end apart: 4 -> 10, of which waited for: 4 -> 9; matrix products, arithmetic and copies ran while one was open for 0% -> 0% of each run, Pallas kernels for 0% -> 0%
where the time goes in v2:
time: 43.2 us; the launch traced here: 43.1 us
  starting transfers between devices  18.5 us (43%)
  waiting for transfers between devices  12.4 us (29%)
  Pallas kernels  10.8 us (25%)
  between operations  1.32 us (3%)
    ppermute x6, starting transfers between devices, exchange(): got[d] = lax.ppermute(sent[d], 'dom', ahead_by(d + 1))  15.4 us
    pallas_call x3, Pallas kernels, call(): pl.pallas_call(kernel, name=name, in_specs=[ANY if hbm_in else VM] * len(...  10.8 us
    ppermute x6, waiting for transfers between devices, exchange(): got[d] = lax.ppermute(sent[d], 'dom', ahead_by(d + 1))  8.23 us
    ppermute x2, waiting for transfers between devices, exchange(): back = lax.ppermute(jnp.concatenate(rest), 'dom', SIBLING)  2.09 us
    ppermute x2, waiting for transfers between devices, exchange(): sibling = lax.ppermute(swap, 'dom', SIBLING)  2.04 us
    ppermute x2, starting transfers between devices, exchange(): sibling = lax.ppermute(swap, 'dom', SIBLING)  1.74 us
    ppermute x2, starting transfers between devices, exchange(): back = lax.ppermute(jnp.concatenate(rest), 'dom', SIBLING)  1.41 us
  transfers between devices with their start and end apart: 10, of which 9 were waited for; matrix products, arithmetic and copies ran while one was open for 0% of the time, Pallas kernels for 0%

profile of v2, /device:TPU:1, one launch (start us, length us, event | category | flops | bytes accessed | tf_op | source)
XLA Modules:
  0.0 43.1 jit_solution(537015674057135662)
XLA Ops:
  1.3 3.7 %predict.1 = (f32[48,384]{1,0:T(8,128)S(1)}, f32[56,384]{1,0:T(8,128)S(1)}, f32[24,1152]{1,0:T(8,128)S(1)}, f32[24,1152]{1,0:T(8,128)S(1)}, f32[24,2304]{1,0:T(8...) custom-call(f32[9,20,128]{2,1,0:T(8,128)} %bitcast.41, ...), custom_call_target="tpu_custom_call" | custom-call | flops 2000000000 | bytes 2000000 | tf_op jit(solution)/shard_map/predict/pallas_call | solution.py:449
  5.0 1.5 %collective-permute-start = (f32[56,384]{1,0:T(8,128)S(1)}, f32[56,384]{1,0:T(8,128)S(1)}, u32[]{:S(2)}, u32[]{:S(2)}) collective-permute-start(f32[56,384]{1,0:T(8,128)S(1)} %get-tuple-element.37), channel_id=1, source_target_pairs={{0,1},{1,0},{2,3},{3,2},{4,5},{5,4},{6,7},{7,6},{8,9},{9,8},{10,11... | collective-permute-start | bytes 258056 | tf_op jit(solution)/shard_map/ppermute | solution.py:470
  6.5 0.9 %collective-permute-done.sibling = f32[56,384]{1,0:T(8,128)S(1)} collective-permute-done((f32[56,384]{1,0:T(8,128)S(1)}, f32[56,384]{1,0:T(8,128)S(1)}, u32[]{:S(2)}, u32[]{:S(2)}) %collective-permute-start) | collective-permute-done | bytes 86048 | tf_op jit(solution)/shard_map/ppermute | solution.py:470
  7.5 8.6 %collective-permute-start.1 = (f32[32,384]{1,0:T(8,128)S(1)}, f32[32,384]{1,0:T(8,128)S(1)}, u32[]{:S(2)}, u32[]{:S(2)}) collective-permute-start(f32[32,384]{1,0:T(8,128)S(1)} %pad_maximum_fusion.2), channel_id=1, source_target_pairs={{0,2},{1,127},{2,4},{3,1},{4,6},{5,3},{6,8},{7,5},{8,10},{9,7},{10... | collective-permute-start | bytes 147464 | tf_op jit(solution)/shard_map/ppermute | solution.py:474
  16.0 0.5 %collective-permute-start.2 = (f32[32,384]{1,0:T(8,128)S(1)}, f32[32,384]{1,0:T(8,128)S(1)}, u32[]{:S(2)}, u32[]{:S(2)}) collective-permute-start(f32[32,384]{1,0:T(8,128)S(1)} %pad_maximum_fusion.3), channel_id=1, source_target_pairs={{0,4},{1,125},{2,6},{3,127},{4,8},{5,1},{6,10},{7,3},{8,12},{9,5},... | collective-permute-start | bytes 147464 | tf_op jit(solution)/shard_map/ppermute | solution.py:474
  16.5 0.8 %collective-permute-start.3 = (f32[32,384]{1,0:T(8,128)S(1)}, f32[32,384]{1,0:T(8,128)S(1)}, u32[]{:S(2)}, u32[]{:S(2)}) collective-permute-start(f32[32,384]{1,0:T(8,128)S(1)} %pad_maximum_fusion.4), channel_id=1, source_target_pairs={{0,6},{1,123},{2,8},{3,125},{4,10},{5,127},{6,12},{7,1},{8,14},{9,... | collective-permute-start | bytes 147464 | tf_op jit(solution)/shard_map/ppermute | solution.py:474
  17.3 0.0 collective-permute-done.1.got_1
  17.3 3.2 %collective-permute-done.2.got_2 = f32[32,384]{1,0:T(8,128)S(1)} collective-permute-done((f32[32,384]{1,0:T(8,128)S(1)}, f32[32,384]{1,0:T(8,128)S(1)}, u32[]{:S(2)}, u32[]{:S(2)}) %collective-permute-start.2) | collective-permute-done | bytes 49184 | tf_op jit(solution)/shard_map/ppermute | solution.py:474
  20.5 0.5 %collective-permute-done.3.got_3 = f32[32,384]{1,0:T(8,128)S(1)} collective-permute-done((f32[32,384]{1,0:T(8,128)S(1)}, f32[32,384]{1,0:T(8,128)S(1)}, u32[]{:S(2)}, u32[]{:S(2)}) %collective-permute-start.3) | collective-permute-done | bytes 49184 | tf_op jit(solution)/shard_map/ppermute | solution.py:474
  21.0 0.2 collective-permute-start.4
  21.2 1.2 %collective-permute-done.4.back = f32[48,384]{1,0:T(8,128)S(1)} collective-permute-done((f32[48,384]{1,0:T(8,128)S(1)}, f32[48,384]{1,0:T(8,128)S(1)}, u32[]{:S(2)}, u32[]{:S(2)}) %collective-permute-start.4) | collective-permute-done | bytes 73760 | tf_op jit(solution)/shard_map/ppermute | solution.py:476
  22.4 2.5 %substep.1 = (f32[48,384]{1,0:T(8,128)S(1)}, f32[56,384]{1,0:T(8,128)S(1)}, f32[24,1152]{1,0:T(8,128)S(1)}, f32[24,1152]{1,0:T(8,128)S(1)}, f32[32,1152]{1,0:T(8...) custom-call(f32[32,384]{1,0:T(8,128)S(1)} %collective-permute-done.1.got_1, ...), custom_call_target="tpu_custom_call" | custom-call | flops 2000000000 | bytes 2000000 | tf_op jit(solution)/shard_map/substep/pallas_call | solution.py:449
  24.9 0.2 collective-permute-start.5
  25.1 1.1 %collective-permute-done.5.sibling = f32[56,384]{1,0:T(8,128)S(1)} collective-permute-done((f32[56,384]{1,0:T(8,128)S(1)}, f32[56,384]{1,0:T(8,128)S(1)}, u32[]{:S(2)}, u32[]{:S(2)}) %collective-permute-start.5) | collective-permute-done | bytes 86048 | tf_op jit(solution)/shard_map/ppermute | solution.py:470
  26.3 4.8 %collective-permute-start.6 = (f32[32,384]{1,0:T(8,128)S(1)}, f32[32,384]{1,0:T(8,128)S(1)}, u32[]{:S(2)}, u32[]{:S(2)}) collective-permute-start(f32[32,384]{1,0:T(8,128)S(1)} %pad_maximum_fusion.5), channel_id=1, source_target_pairs={{0,2},{1,127},{2,4},{3,1},{4,6},{5,3},{6,8},{7,5},{8,10},{9,7},{10... | collective-permute-start | bytes 147464 | tf_op jit(solution)/shard_map/ppermute | solution.py:474
  31.1 0.7 %collective-permute-start.7 = (f32[32,384]{1,0:T(8,128)S(1)}, f32[32,384]{1,0:T(8,128)S(1)}, u32[]{:S(2)}, u32[]{:S(2)}) collective-permute-start(f32[32,384]{1,0:T(8,128)S(1)} %pad_maximum_fusion.6), channel_id=1, source_target_pairs={{0,4},{1,125},{2,6},{3,127},{4,8},{5,1},{6,10},{7,3},{8,12},{9,5},... | collective-permute-start | bytes 147464 | tf_op jit(solution)/shard_map/ppermute | solution.py:474
  31.8 0.0 collective-permute-start.8
  31.8 0.5 %collective-permute-done.6.got_1 = f32[32,384]{1,0:T(8,128)S(1)} collective-permute-done((f32[32,384]{1,0:T(8,128)S(1)}, f32[32,384]{1,0:T(8,128)S(1)}, u32[]{:S(2)}, u32[]{:S(2)}) %collective-permute-start.6) | collective-permute-done | bytes 49184 | tf_op jit(solution)/shard_map/ppermute | solution.py:474
  32.3 3.6 %collective-permute-done.7.got_2 = f32[32,384]{1,0:T(8,128)S(1)} collective-permute-done((f32[32,384]{1,0:T(8,128)S(1)}, f32[32,384]{1,0:T(8,128)S(1)}, u32[]{:S(2)}, u32[]{:S(2)}) %collective-permute-start.7) | collective-permute-done | bytes 49184 | tf_op jit(solution)/shard_map/ppermute | solution.py:474
  35.8 0.5 %collective-permute-done.8.got_3 = f32[32,384]{1,0:T(8,128)S(1)} collective-permute-done((f32[32,384]{1,0:T(8,128)S(1)}, f32[32,384]{1,0:T(8,128)S(1)}, u32[]{:S(2)}, u32[]{:S(2)}) %collective-permute-start.8) | collective-permute-done | bytes 49184 | tf_op jit(solution)/shard_map/ppermute | solution.py:474
  36.4 1.2 %collective-permute-start.9 = (f32[48,384]{1,0:T(8,128)S(1)}, f32[48,384]{1,0:T(8,128)S(1)}, u32[]{:S(2)}, u32[]{:S(2)}) collective-permute-start(f32[48,384]{1,0:T(8,128)S(1)} %pad_maximum_fusion.1), channel_id=1, source_target_pairs={{0,1},{1,0},{2,3},{3,2},{4,5},{5,4},{6,7},{7,6},{8,9},{9,8},{10,11... | collective-permute-start | bytes 221192 | tf_op jit(solution)/shard_map/ppermute | solution.py:476
  37.6 0.9 %collective-permute-done.9.back = f32[48,384]{1,0:T(8,128)S(1)} collective-permute-done((f32[48,384]{1,0:T(8,128)S(1)}, f32[48,384]{1,0:T(8,128)S(1)}, u32[]{:S(2)}, u32[]{:S(2)}) %collective-permute-start.9) | collective-permute-done | bytes 73760 | tf_op jit(solution)/shard_map/ppermute | solution.py:476
  38.5 4.5 %finish.1 = (f32[9,20,128]{2,1,0:T(8,128)}, f32[9,20,256]{2,1,0:T(8,128)}) custom-call(f32[32,384]{1,0:T(8,128)S(1)} %collective-permute-done.6.got_1, f32[32,384]{1,0:T(8,128)S(1)} %collective-permute-done.7.got_2, f32[32,384]{1,0:T(8,128)S(1)} %collective-permute-done.8.got_3, f32[48,384]{1,0:T(8,128)S(1)} %collective-permute-done.9.back, ...), custom_call_target="tpu_custom_call" | custom-call | flops 2000000000 | bytes 2000000 | tf_op jit(solution)/shard_map/finish/pallas_call | solution.py:449
  (18 shorter events, 0.1 us)
Async XLA Ops:
  5.0 2.4 %collective-permute-start = (f32[56,384]{1,0:T(8,128)S(1)}, f32[56,384]{1,0:T(8,128)S(1)}, u32[]{:S(2)}, u32[]{:S(2)}) collective-permute-start(f32[56,384]{1,0:T(8,128)S(1)} %get-tuple-element.37), channel_id=1, source_target_pairs={{0,1},{1,0},{2,3},{3,2},{4,5},{5,4},{6,7},{7,6},{8,9},{9,8},{10,11... | collective-permute-start | bytes 258056 | tf_op jit(solution)/shard_map/ppermute | solution.py:470
  7.5 9.9 %collective-permute-start.1 = (f32[32,384]{1,0:T(8,128)S(1)}, f32[32,384]{1,0:T(8,128)S(1)}, u32[]{:S(2)}, u32[]{:S(2)}) collective-permute-start(f32[32,384]{1,0:T(8,128)S(1)} %pad_maximum_fusion.2), channel_id=1, source_target_pairs={{0,2},{1,127},{2,4},{3,1},{4,6},{5,3},{6,8},{7,5},{8,10},{9,7},{10... | collective-permute-start | bytes 147464 | tf_op jit(solution)/shard_map/ppermute | solution.py:474
  16.0 4.5 %collective-permute-start.2 = (f32[32,384]{1,0:T(8,128)S(1)}, f32[32,384]{1,0:T(8,128)S(1)}, u32[]{:S(2)}, u32[]{:S(2)}) collective-permute-start(f32[32,384]{1,0:T(8,128)S(1)} %pad_maximum_fusion.3), channel_id=1, source_target_pairs={{0,4},{1,125},{2,6},{3,127},{4,8},{5,1},{6,10},{7,3},{8,12},{9,5},... | collective-permute-start | bytes 147464 | tf_op jit(solution)/shard_map/ppermute | solution.py:474
  16.5 4.4 %collective-permute-start.3 = (f32[32,384]{1,0:T(8,128)S(1)}, f32[32,384]{1,0:T(8,128)S(1)}, u32[]{:S(2)}, u32[]{:S(2)}) collective-permute-start(f32[32,384]{1,0:T(8,128)S(1)} %pad_maximum_fusion.4), channel_id=1, source_target_pairs={{0,6},{1,123},{2,8},{3,125},{4,10},{5,127},{6,12},{7,1},{8,14},{9,... | collective-permute-start | bytes 147464 | tf_op jit(solution)/shard_map/ppermute | solution.py:474
  21.0 1.3 %collective-permute-start.4 = (f32[48,384]{1,0:T(8,128)S(1)}, f32[48,384]{1,0:T(8,128)S(1)}, u32[]{:S(2)}, u32[]{:S(2)}) collective-permute-start(f32[48,384]{1,0:T(8,128)S(1)} %pad_maximum_fusion), channel_id=1, source_target_pairs={{0,1},{1,0},{2,3},{3,2},{4,5},{5,4},{6,7},{7,6},{8,9},{9,8},{10,11... | collective-permute-start | bytes 221192 | tf_op jit(solution)/shard_map/ppermute | solution.py:476
  24.9 1.4 %collective-permute-start.5 = (f32[56,384]{1,0:T(8,128)S(1)}, f32[56,384]{1,0:T(8,128)S(1)}, u32[]{:S(2)}, u32[]{:S(2)}) collective-permute-start(f32[56,384]{1,0:T(8,128)S(1)} %get-tuple-element.55), channel_id=1, source_target_pairs={{0,1},{1,0},{2,3},{3,2},{4,5},{5,4},{6,7},{7,6},{8,9},{9,8},{10,11... | collective-permute-start | bytes 258056 | tf_op jit(solution)/shard_map/ppermute | solution.py:470
  26.3 6.0 %collective-permute-start.6 = (f32[32,384]{1,0:T(8,128)S(1)}, f32[32,384]{1,0:T(8,128)S(1)}, u32[]{:S(2)}, u32[]{:S(2)}) collective-permute-start(f32[32,384]{1,0:T(8,128)S(1)} %pad_maximum_fusion.5), channel_id=1, source_target_pairs={{0,2},{1,127},{2,4},{3,1},{4,6},{5,3},{6,8},{7,5},{8,10},{9,7},{10... | collective-permute-start | bytes 147464 | tf_op jit(solution)/shard_map/ppermute | solution.py:474
  31.1 4.7 %collective-permute-start.7 = (f32[32,384]{1,0:T(8,128)S(1)}, f32[32,384]{1,0:T(8,128)S(1)}, u32[]{:S(2)}, u32[]{:S(2)}) collective-permute-start(f32[32,384]{1,0:T(8,128)S(1)} %pad_maximum_fusion.6), channel_id=1, source_target_pairs={{0,4},{1,125},{2,6},{3,127},{4,8},{5,1},{6,10},{7,3},{8,12},{9,5},... | collective-permute-start | bytes 147464 | tf_op jit(solution)/shard_map/ppermute | solution.py:474
  31.8 4.6 %collective-permute-start.8 = (f32[32,384]{1,0:T(8,128)S(1)}, f32[32,384]{1,0:T(8,128)S(1)}, u32[]{:S(2)}, u32[]{:S(2)}) collective-permute-start(f32[32,384]{1,0:T(8,128)S(1)} %pad_maximum_fusion.7), channel_id=1, source_target_pairs={{0,6},{1,123},{2,8},{3,125},{4,10},{5,127},{6,12},{7,1},{8,14},{9,... | collective-permute-start | bytes 147464 | tf_op jit(solution)/shard_map/ppermute | solution.py:474
  36.4 2.2 %collective-permute-start.9 = (f32[48,384]{1,0:T(8,128)S(1)}, f32[48,384]{1,0:T(8,128)S(1)}, u32[]{:S(2)}, u32[]{:S(2)}) collective-permute-start(f32[48,384]{1,0:T(8,128)S(1)} %pad_maximum_fusion.1), channel_id=1, source_target_pairs={{0,1},{1,0},{2,3},{3,2},{4,5},{5,4},{6,7},{7,6},{8,9},{9,8},{10,11... | collective-permute-start | bytes 221192 | tf_op jit(solution)/shard_map/ppermute | solution.py:476

commit v3 on v2

--- a/solution.py
+++ b/solution.py
@@ -164,7 +164,7 @@
     parts = []
     for ref in direct:
         parts += [ref[0:8], ref[16:24]]
-    parts += [back[...], sibling[KEPT : KEPT + 8], jnp.zeros((LANES - BLOCKS * 8, ROW), F32)]
+    parts += [back[0:KEPT], sibling[KEPT : KEPT + 8], jnp.zeros((LANES - BLOCKS * 8, ROW), F32)]
     rows = jnp.concatenate(parts, axis=0)
     turned = [rows[:, t * LANES : (t + 1) * LANES].T for t in range(3)]
     fine = jnp.concatenate(turned[:2], axis=0)
@@ -280,9 +280,47 @@
     return [(number & (1 << k)) != 0 for k in range(count)]
 
 
-def correct(
-    state_ref, width, own_ref, tables, neighbors, faces, turns, star_ref, flux_ref, w_rot, w_lift,
-    t_ref, n_ref, l_ref, emit,
+def at_face(tables, firsts, q, at, numbers):
+    found = []
+    for (ref, width, tile), first in zip(tables, firsts):
+        start = first(q) * width + tile * LANES
+        found.append(pick([
+            jnp.take_along_axis(ref[f * FP : (f + 1) * FP, start : start + LANES], at, axis=1)
+            for f in range(4)
+        ], numbers))
+    return found
+
+
+def near_part(
+    state_ref, width, own_ref, tables, neighbors, faces, star_ref, flux_ref, t_ref,
+    base_ref, side_ref, near_ref,
+):
+    for tile in range(width // LANES):
+        lanes = slice(tile * LANES, (tile + 1) * LANES)
+        for i in range(4):
+            kind, lane = locate(spread(neighbors, i, tile))
+            kinds = bits_of(kind, 2)
+            numbers = bits_of(spread(faces, i, tile), 2)
+            acc = [None] * NQ
+            for q in range(NQ):
+                start = q * width + tile * LANES
+                found = at_face(tables, [lambda q: q] * 3, q, lane, numbers)
+                near_ref[i, :, start : start + LANES] = pick(found, kinds)
+                own = own_ref[i * FP : (i + 1) * FP, start : start + LANES]
+                for p in range(NQ):
+                    term = own * flux_ref[0, q, p, i : i + 1, lanes]
+                    acc[p] = term if acc[p] is None else acc[p] + term
+            for p in range(NQ):
+                start = p * width + tile * LANES
+                side_ref[i * FP : (i + 1) * FP, start : start + LANES] = acc[p]
+        volume = star_sum(t_ref, star_ref, width, tile)
+        state = get(state_ref, width, tile)
+        put(base_ref, [s + v for s, v in zip(state, volume)], width, tile)
+
+
+def far_part(
+    width, ghosts, neighbors, faces, turns, flux_ref, w_rot, w_lift,
+    base_ref, side_ref, near_ref, n_ref, l_ref, emit,
 ):
     turned = [
         [jnp.broadcast_to(w_rot[h * FP : (h + 1) * FP, b : b + 1], (FP, LANES)) for h in range(3)]
@@ -293,72 +331,98 @@
         for i in range(4):
             kind, lane = locate(spread(neighbors, i, tile))
             later = jnp.where(kind == 4, lane + 4, lane)
-            face = spread(faces, i, tile)
-            turn = spread(turns, i, tile)
-            kinds = bits_of(kind, 3)
-            numbers = bits_of(face, 2)
+            fine, local = kind == 3, kind < 3
+            numbers = bits_of(spread(faces, i, tile), 2)
             for q in range(NQ):
-                at = lane if q < 5 else later
-                found = []
-                for k, (ref, ref_width, ref_tile) in enumerate(tables):
-                    start = (q if k < 4 else q % 5) * ref_width + ref_tile * LANES
-                    found.append(pick([
-                        jnp.take_along_axis(
-                            ref[f * FP : (f + 1) * FP, start : start + LANES], at, axis=1
-                        )
-                        for f in range(4)
-                    ], numbers))
-                n_ref[i, :, q * LANES : (q + 1) * LANES] = pick(found, kinds)
-            turn_by = [pick(turned[b], bits_of(turn, 2)) for b in range(FNB)]
-            acc = [None] * NQ
+                start = q * width + tile * LANES
+                found = at_face(
+                    ghosts, [lambda q: q, lambda q: q % 5], q, lane if q < 5 else later, numbers
+                )
+                ghost = jnp.where(fine, found[0], found[1])
+                n_ref[i, :, q * LANES : (q + 1) * LANES] = jnp.where(
+                    local, near_ref[i, :, start : start + LANES], ghost
+                )
+            ways = bits_of(spread(turns, i, tile), 2)
+            turn_by = [pick(turned[b], ways) for b in range(FNB)]
+            acc = []
+            for p in range(NQ):
+                start = p * width + tile * LANES
+                acc.append(side_ref[i * FP : (i + 1) * FP, start : start + LANES])
             for q in range(NQ):
                 at = slice(q * LANES, (q + 1) * LANES)
                 other = turn_by[0] * n_ref[i, 0:1, at]
                 for b in range(1, FNB):
                     other = other + turn_by[b] * n_ref[i, b : b + 1, at]
-                start = q * width + tile * LANES
-                own = own_ref[i * FP : (i + 1) * FP, start : start + LANES]
                 for p in range(NQ):
-                    term = own * flux_ref[0, q, p, i : i + 1, lanes]
-                    term = term + other * flux_ref[1, q, p, i : i + 1, lanes]
-                    acc[p] = term if acc[p] is None else acc[p] + term
+                    acc[p] = acc[p] + other * flux_ref[1, q, p, i : i + 1, lanes]
             for p in range(NQ):
                 l_ref[i * FP : (i + 1) * FP, p * LANES : (p + 1) * LANES] = acc[p]
         lifted = mm(w_lift, l_ref[...])
-        volume = star_sum(t_ref, star_ref, width, tile)
-        state = get(state_ref, width, tile)
-        emit(
-            tile,
-            [state[p] + (volume[p] + lifted[:, p * LANES : (p + 1) * LANES]) for p in range(NQ)],
-        )
-
-
-def second_kernel(
-    got_1, got_2, got_3, back, sibling, x_fine, i_fine, c_first, c_second, star_f, flux_f,
-    neighbors, faces, turns, send_fine, send_coarse, w_time, w_vol, w_proj, w_rot, w_lift, count,
-    keep, swap, x_next, i_next, p_own, p_coarse, p_gf, p_gc,
-    ghost_f, ghost_c, t_ref, n_ref, l_ref, d_ref,
-):
+        base = get(base_ref, width, tile)
+        emit(tile, [base[p] + lifted[:, p * LANES : (p + 1) * LANES] for p in range(NQ)])
+
+
+def near_fine_kernel(
+    sibling, x_fine, i_fine, c_first, star_f, flux_f, neighbors, faces, w_vol, w_proj,
+    base, side, near, p_own, p_coarse, spare,
+    t_ref,
+):
+    spare[...] = sibling[KEPT : KEPT + 8]
     w_v, w_p = weight(w_vol, BP), weight(w_proj, BP)
     t_ref[...] = mm(w_v, i_fine[...])
     p_own[...] = mm(w_p, i_fine[...])
     p_coarse[...] = mm(w_p, c_first[...])
+    tables = [(p_own, LANES, 0), (p_coarse, 2 * LANES, 0), (p_coarse, 2 * LANES, 1)]
+    near_part(
+        x_fine, LANES, p_own, tables, neighbors, faces, star_f, flux_f, t_ref, base, side, near,
+    )
+
+
+def near_last_kernel(
+    sibling, x_fine, i_fine, x_coarse, c_first, c_second, p_own, p_coarse,
+    fine_star, fine_flux, coarse_star, coarse_flux, neighbors, faces, c_neighbors, c_faces,
+    w_vol, w_proj,
+    base_f, side_f, near_f, base_c, side_c, near_c, spare,
+    q_own, q_coarse, t_ref, tc_ref,
+):
+    spare[...] = sibling[KEPT : KEPT + 8]
+    w_v, w_p = weight(w_vol, BP), weight(w_proj, BP)
+    t_ref[...] = mm(w_v, i_fine[...])
+    q_own[...] = mm(w_p, i_fine[...])
+    q_coarse[...] = mm(w_p, c_second[...])
+    tc_ref[...] = mm(w_v, c_first[...] + c_second[...])
+    tables = [(q_own, LANES, 0), (q_coarse, 2 * LANES, 0), (q_coarse, 2 * LANES, 1)]
+    near_part(
+        x_fine, LANES, q_own, tables, neighbors, faces, fine_star, fine_flux, t_ref,
+        base_f, side_f, near_f,
+    )
+    q_own[...] = q_own[...] + p_own[...]
+    q_coarse[...] = q_coarse[...] + p_coarse[...]
+    near_part(
+        x_coarse, 2 * LANES, q_coarse, tables, c_neighbors, c_faces, coarse_star, coarse_flux,
+        tc_ref, base_c, side_c, near_c,
+    )
+
+
+def second_kernel(
+    got_1, got_2, got_3, back, sibling, x_fine, base, side, near, c_second, star_f, flux_f,
+    neighbors, faces, turns, send_fine, send_coarse, w_time, w_proj, w_rot, w_lift, count,
+    keep, swap, x_next, i_next, p_gf, p_gc,
+    ghost_f, ghost_c, t_ref, n_ref, l_ref, d_ref,
+):
+    w_p = weight(w_proj, BP)
     unpack((got_1, got_2, got_3, back, sibling), ghost_f, ghost_c)
     p_gf[...] = mm(w_p, ghost_f[...])
     p_gc[...] = mm(w_p, ghost_c[...])
     live = lax.broadcasted_iota(I32, (BP, LANES), 1) < count[0]
-    tables = [
-        (p_own, LANES, 0), (p_coarse, 2 * LANES, 0), (p_coarse, 2 * LANES, 1),
-        (p_gf, LANES, 0), (p_gc, LANES, 0),
-    ]
 
     def emit_state(tile, values):
         old = get(x_fine, LANES, 0)
         put(x_next, [jnp.where(live, v, o) for v, o in zip(values, old)], LANES, 0)
 
-    correct(
-        x_fine, LANES, p_own, tables, neighbors, faces, turns, star_f, flux_f,
-        w_rot, weight(w_lift, 32), t_ref, n_ref, l_ref, emit_state,
+    far_part(
+        LANES, [(p_gf, LANES, 0), (p_gc, LANES, 0)], neighbors, faces, turns, flux_f,
+        w_rot, weight(w_lift, 32), base, side, near, n_ref, l_ref, emit_state,
     )
 
     def emit_fine(tile, *terms):
@@ -374,48 +438,40 @@
 
 
 def third_kernel(
-    got_1, got_2, got_3, back, sibling, x_fine, i_fine, x_coarse, c_first, c_second, p_own, p_coarse, p_gf, p_gc,
-    fine_star, fine_flux, coarse_star, coarse_flux,
-    neighbors, faces, turns, c_neighbors, c_faces, c_turns, w_vol, w_proj, w_rot, w_lift, count,
+    got_1, got_2, got_3, back, sibling, x_fine, base_f, side_f, near_f, base_c, side_c, near_c,
+    p_gf, p_gc, fine_flux, coarse_flux, neighbors, faces, turns, c_neighbors, c_faces, c_turns,
+    w_proj, w_rot, w_lift, count,
     fine_out, coarse_out,
-    q_own, q_coarse, q_gf, q_gc, ghost_f, ghost_c, t_ref, tc_ref, n_ref, l_ref,
-    fine_v, coarse_v, sems,
-):
-    w_v, w_p, w_l = weight(w_vol, BP), weight(w_proj, BP), weight(w_lift, 32)
-    t_ref[...] = mm(w_v, i_fine[...])
-    q_own[...] = mm(w_p, i_fine[...])
-    q_coarse[...] = mm(w_p, c_second[...])
-    tc_ref[...] = mm(w_v, c_first[...] + c_second[...])
+    q_gf, q_gc, ghost_f, ghost_c, n_ref, l_ref, fine_v, coarse_v, sems,
+):
+    w_p, w_l = weight(w_proj, BP), weight(w_lift, 32)
     unpack((got_1, got_2, got_3, back, sibling), ghost_f, ghost_c)
     q_gf[...] = mm(w_p, ghost_f[...])
     q_gc[...] = mm(w_p, ghost_c[...])
     live = lax.broadcasted_iota(I32, (NB, LANES), 1) < count[0]
-    tables = [
-        (q_own, LANES, 0), (q_coarse, 2 * LANES, 0), (q_coarse, 2 * LANES, 1),
-        (q_gf, LANES, 0), (q_gc, LANES, 0),
-    ]
+    ghosts = [(q_gf, LANES, 0), (q_gc, LANES, 0)]
 
     def emit_fine(tile, values):
         old = get(x_fine, LANES, 0)
         for p in range(NQ):
             fine_v[p] = jnp.where(live, values[p][:NB], old[p][:NB])
 
-    correct(
-        x_fine, LANES, q_own, tables, neighbors, faces, turns, fine_star, fine_flux,
-        w_rot, w_l, t_ref, n_ref, l_ref, emit_fine,
+    far_part(
+        LANES, ghosts, neighbors, faces, turns, fine_flux, w_rot, w_l,
+        base_f, side_f, near_f, n_ref, l_ref, emit_fine,
     )
     fine_copy = pltpu.make_async_copy(fine_v, fine_out, sems.at[0])
     fine_copy.start()
-    for total, prior in ((q_own, p_own), (q_coarse, p_coarse), (q_gf, p_gf), (q_gc, p_gc)):
-        total[...] = total[...] + prior[...]
+    q_gf[...] = q_gf[...] + p_gf[...]
+    q_gc[...] = q_gc[...] + p_gc[...]
 
     def emit_coarse(tile, values):
         for p in range(NQ):
             coarse_v[p, :, tile * LANES : (tile + 1) * LANES] = values[p][:NB]
 
-    correct(
-        x_coarse, 2 * LANES, q_coarse, tables, c_neighbors, c_faces, c_turns, coarse_star,
-        coarse_flux, w_rot, w_l, tc_ref, n_ref, l_ref, emit_coarse,
+    far_part(
+        2 * LANES, ghosts, c_neighbors, c_faces, c_turns, coarse_flux, w_rot, w_l,
+        base_c, side_c, near_c, n_ref, l_ref, emit_coarse,
     )
     coarse_copy = pltpu.make_async_copy(coarse_v, coarse_out, sems.at[1])
     coarse_copy.start()
@@ -436,6 +492,7 @@
 GHOST_C = (BP, 5 * LANES)
 FACES_G = (4 * FP, 5 * LANES)
 PICKED = (4, FP, NQ * LANES)
+PICKED_C = (4, FP, 2 * NQ * LANES)
 WEIGHTS = [(3 * BP, LANES), (4 * FP, LANES), (3 * FP, LANES), (BP, LANES)]
 PARAMS = pltpu.CompilerParams(vmem_limit_bytes=24 * 1024 * 1024)
 
@@ -462,18 +519,20 @@
 
 
 def ahead_by(distance):
-    step = 2 * distance
-    return [(i, (i + (step if i % 2 == 0 else -step)) % N_DEV) for i in range(N_DEV)]
-
-
-def exchange(keep, swap):
-    sibling = lax.ppermute(swap, "dom", SIBLING)
+    pairs = []
+    for i in range(N_DEV):
+        target = i + (2 * distance if i % 2 == 0 else -2 * distance)
+        pairs.append((i, target if 0 <= target < N_DEV else i ^ 1))
+    return pairs
+
+
+def exchange(keep, sibling, spare):
     sent = [jnp.concatenate([keep[16 * d : 16 * d + 16], sibling[16 * d : 16 * d + 16]]) for d in range(3)]
     got = [None] * 3
     for d in (2, 1, 0):
         got[d] = lax.ppermute(sent[d], "dom", ahead_by(d + 1))
     rest = [g.reshape(2, 2, 8, ROW)[:, 1].reshape(16, ROW) for g in got]
-    back = lax.ppermute(jnp.concatenate(rest), "dom", SIBLING)
+    back = lax.ppermute(jnp.concatenate(rest + [spare]), "dom", SIBLING)
     return *got, back, sibling
 
 
@@ -507,22 +566,36 @@
         count, hbm_in=True, sems=19,
     )
     links, (w_time, *weights) = rest[:6], rest[6:]
-    arrived = exchange(keep, swap)
-    keep, swap, x_next, i_second, *tables = call(
+    w_vol, w_proj, w_rot, w_lift = weights
+    sibling = lax.ppermute(swap, "dom", SIBLING)
+    base, side, near, p_own, p_coarse, spare = call(
+        near_fine_kernel, "near_fine", [FINE, FACES_F, PICKED, FACES_F, FACES_C, (8, ROW)], [STIFF_F],
+        (sibling, x_fine, i_first, c_first, fine_star, fine_flux, *links[:2], w_vol, w_proj), (), us=1,
+    )
+    arrived = exchange(keep, sibling, spare)
+    keep, swap, x_next, i_second, p_gf, p_gc = call(
         second_kernel, "substep",
-        [(KEPT, ROW), (KEPT + 8, ROW), FINE, FINE, FACES_F, FACES_C, FACES_F, FACES_G],
+        [(KEPT, ROW), (KEPT + 8, ROW), FINE, FINE, FACES_F, FACES_G],
         [FINE, GHOST_C, STIFF_F, PICKED, FACES_F, FINE],
-        (*arrived, x_fine, i_first, c_first, c_second, fine_star, fine_flux, *links[:3],
-         send_fine, send_coarse, w_time, *weights), count,
-    )
-    arrived = exchange(keep, swap)
+        (*arrived, x_fine, base, side, near, c_second, fine_star, fine_flux, *links[:3],
+         send_fine, send_coarse, w_time, w_proj, w_rot, w_lift), count,
+    )
+    sibling = lax.ppermute(swap, "dom", SIBLING)
+    *near_parts, spare = call(
+        near_last_kernel, "near_last",
+        [FINE, FACES_F, PICKED, COARSE, FACES_C, PICKED_C, (8, ROW)],
+        [FACES_F, FACES_C, STIFF_F, STIFF_C],
+        (sibling, x_next, i_second, x_coarse, c_first, c_second, p_own, p_coarse,
+         fine_star, fine_flux, coarse_star, coarse_flux, *links[:2], *links[3:5], w_vol, w_proj),
+        (), us=2,
+    )
+    arrived = exchange(keep, sibling, spare)
     results = call(
         third_kernel, "finish",
         [(NQ, NB, LANES), (NQ, NB, 2 * LANES)],
-        [FACES_F, FACES_C, FACES_F, FACES_G, FINE, GHOST_C, STIFF_F, STIFF_C, PICKED, FACES_F,
-         (NQ, NB, LANES), (NQ, NB, 2 * LANES)],
-        (*arrived, x_next, i_second, x_coarse, c_first, c_second, *tables,
-         fine_star, fine_flux, coarse_star, coarse_flux, *links, *weights), count,
+        [FACES_F, FACES_G, FINE, GHOST_C, PICKED, FACES_F, (NQ, NB, LANES), (NQ, NB, 2 * LANES)],
+        (*arrived, x_next, *near_parts, p_gf, p_gc, fine_flux, coarse_flux, *links,
+         w_proj, w_rot, w_lift), count,
         hbm_out=True, sems=2,
     )
     return tuple(r.transpose(1, 0, 2) for r in results)

time: 43.2 us -> 37.2 us (0.86)
  the two profiles are of different devices: /device:TPU:1 before, /device:TPU:97 now
where the time goes in v3:
time: 37.2 us; the launch traced here: 37 us
  starting transfers between devices  15.2 us (41%)
  Pallas kernels  12.1 us (33%)
  waiting for transfers between devices  8.31 us (22%)
  between operations  1.37 us (4%)
    pallas_call x5, Pallas kernels, call(): pl.pallas_call(kernel, name=name, in_specs=[ANY if hbm_in else VM] * len(...  12.1 us
    ppermute x6, starting transfers between devices, exchange(): got[d] = lax.ppermute(sent[d], 'dom', ahead_by(d + 1))  9.41 us
    ppermute x6, waiting for transfers between devices, exchange(): got[d] = lax.ppermute(sent[d], 'dom', ahead_by(d + 1))  4.61 us
    ppermute x2, starting transfers between devices, exchange(): back = lax.ppermute(jnp.concatenate(rest + [spare]), 'dom', SIBLING)  4.56 us
    ppermute x2, waiting for transfers between devices, exchange(): back = lax.ppermute(jnp.concatenate(rest + [spare]), 'dom', SIBLING)  1.86 us
    ppermute x2, waiting for transfers between devices, local(): sibling = lax.ppermute(swap, 'dom', SIBLING)  1.84 us
    ppermute x2, starting transfers between devices, local(): sibling = lax.ppermute(swap, 'dom', SIBLING)  1.19 us
  transfers between devices with their start and end apart: 10, of which 8 were waited for; matrix products, arithmetic and copies ran while one was open for 0% of the time, Pallas kernels for 10%

profile of v3, /device:TPU:97, one launch (start us, length us, event | category | flops | bytes accessed | tf_op | source)
XLA Modules:
  0.0 37.0 jit_solution(14386879755513330393)
XLA Ops:
  1.3 3.7 %predict.1 = (f32[48,384]{1,0:T(8,128)S(1)}, f32[56,384]{1,0:T(8,128)S(1)}, f32[24,1152]{1,0:T(8,128)S(1)}, f32[24,1152]{1,0:T(8,128)S(1)}, f32[24,2304]{1,0:T(8...) custom-call(f32[9,20,128]{2,1,0:T(8,128)} %bitcast.41, ...), custom_call_target="tpu_custom_call" | custom-call | flops 2000000000 | bytes 2000000 | tf_op jit(solution)/shard_map/predict/pallas_call | solution.py:506
  5.0 0.8 %collective-permute-start = (f32[56,384]{1,0:T(8,128)S(1)}, f32[56,384]{1,0:T(8,128)S(1)}, u32[]{:S(2)}, u32[]{:S(2)}) collective-permute-start(f32[56,384]{1,0:T(8,128)S(1)} %get-tuple-element.48), channel_id=1, source_target_pairs={{0,1},{1,0},{2,3},{3,2},{4,5},{5,4},{6,7},{7,6},{8,9},{9,8},{10,11... | collective-permute-start | bytes 258056 | tf_op jit(solution)/shard_map/ppermute | solution.py:570
  5.8 0.9 %collective-permute-done.sibling = f32[56,384]{1,0:T(8,128)S(1)} collective-permute-done((f32[56,384]{1,0:T(8,128)S(1)}, f32[56,384]{1,0:T(8,128)S(1)}, u32[]{:S(2)}, u32[]{:S(2)}) %collective-permute-start) | collective-permute-done | bytes 86048 | tf_op jit(solution)/shard_map/ppermute | solution.py:570
  6.7 4.8 %collective-permute-start.1 = (f32[32,384]{1,0:T(8,128)S(1)}, f32[32,384]{1,0:T(8,128)S(1)}, u32[]{:S(2)}, u32[]{:S(2)}) collective-permute-start(f32[32,384]{1,0:T(8,128)S(1)} %pad_maximum_fusion.2), channel_id=1, source_target_pairs={{0,2},{1,0},{2,4},{3,1},{4,6},{5,3},{6,8},{7,5},{8,10},{9,7},{10,1... | collective-permute-start | bytes 147464 | tf_op jit(solution)/shard_map/ppermute | solution.py:533
  11.6 0.5 %collective-permute-start.2 = (f32[32,384]{1,0:T(8,128)S(1)}, f32[32,384]{1,0:T(8,128)S(1)}, u32[]{:S(2)}, u32[]{:S(2)}) collective-permute-start(f32[32,384]{1,0:T(8,128)S(1)} %pad_maximum_fusion.3), channel_id=1, source_target_pairs={{0,4},{1,0},{2,6},{3,2},{4,8},{5,1},{6,10},{7,3},{8,12},{9,5},{10,... | collective-permute-start | bytes 147464 | tf_op jit(solution)/shard_map/ppermute | solution.py:533
  12.1 0.8 %collective-permute-start.3 = (f32[32,384]{1,0:T(8,128)S(1)}, f32[32,384]{1,0:T(8,128)S(1)}, u32[]{:S(2)}, u32[]{:S(2)}) collective-permute-start(f32[32,384]{1,0:T(8,128)S(1)} %pad_maximum_fusion.4), channel_id=1, source_target_pairs={{0,6},{1,0},{2,8},{3,2},{4,10},{5,4},{6,12},{7,1},{8,14},{9,3},{10... | collective-permute-start | bytes 147464 | tf_op jit(solution)/shard_map/ppermute | solution.py:533
  12.9 1.1 %near_fine.1 = (f32[24,1152]{1,0:T(8,128)S(1)}, f32[32,1152]{1,0:T(8,128)S(1)}, f32[4,8,1152]{2,1,0:T(8,128)S(1)}, f32[32,1152]{1,0:T(8,128)S(1)}, f32[32,2304]{1,0:T(8,128)S(1)}, /*index=5*/f32[8,384]{1,0:T(8,128)S(1)}) custom-call(f32[56,384]{1,0:T(8,128)S(1)} %collective-permute-done.sibling, f32[24,1152]{1,0:T(8,128)S(1)} %get-tuple-element.49.x_fine, ...), custom_call_target="tpu_custom_call" | custom-call | flops 1000000000 | bytes 1000000 | tf_op jit(solution)/shard_map/near_fine/pallas_call | solution.py:506
  14.0 0.0 collective-permute-done.1.got_1
  14.0 2.3 %collective-permute-done.2.got_2 = f32[32,384]{1,0:T(8,128)S(1)} collective-permute-done((f32[32,384]{1,0:T(8,128)S(1)}, f32[32,384]{1,0:T(8,128)S(1)}, u32[]{:S(2)}, u32[]{:S(2)}) %collective-permute-start.2) | collective-permute-done | bytes 49184 | tf_op jit(solution)/shard_map/ppermute | solution.py:533
  16.3 0.5 %collective-permute-done.3.got_3 = f32[32,384]{1,0:T(8,128)S(1)} collective-permute-done((f32[32,384]{1,0:T(8,128)S(1)}, f32[32,384]{1,0:T(8,128)S(1)}, u32[]{:S(2)}, u32[]{:S(2)}) %collective-permute-start.3) | collective-permute-done | bytes 49184 | tf_op jit(solution)/shard_map/ppermute | solution.py:533
  16.8 1.7 %collective-permute-start.4 = (f32[56,384]{1,0:T(8,128)S(1)}, f32[56,384]{1,0:T(8,128)S(1)}, u32[]{:S(2)}, u32[]{:S(2)}) collective-permute-start(f32[56,384]{1,0:T(8,128)S(1)} %pad_maximum_fusion), channel_id=1, source_target_pairs={{0,1},{1,0},{2,3},{3,2},{4,5},{5,4},{6,7},{7,6},{8,9},{9,8},{10,11... | collective-permute-start | bytes 258056 | tf_op jit(solution)/shard_map/ppermute | solution.py:535
  18.6 0.9 %collective-permute-done.4.back = f32[56,384]{1,0:T(8,128)S(1)} collective-permute-done((f32[56,384]{1,0:T(8,128)S(1)}, f32[56,384]{1,0:T(8,128)S(1)}, u32[]{:S(2)}, u32[]{:S(2)}) %collective-permute-start.4) | collective-permute-done | bytes 86048 | tf_op jit(solution)/shard_map/ppermute | solution.py:535
  19.5 2.1 %substep.1 = (f32[48,384]{1,0:T(8,128)S(1)}, f32[56,384]{1,0:T(8,128)S(1)}, f32[24,1152]{1,0:T(8,128)S(1)}, f32[24,1152]{1,0:T(8,128)S(1)}, f32[32,1152]{1,0:T(8,128)S(1)}, /*index=5*/f32[32,640]{1,0:T(8,128)S(1)}) custom-call(f32[32,384]{1,0:T(8,128)S(1)} %collective-permute-done.1.got_1, f32[32,384]{1,0:T(8,128)S(1)} %collective-permute-done.2.got_2, ...), custom_call_target="tpu_custom_call" | custom-call | flops 2000000000 | bytes 2000000 | tf_op jit(solution)/shard_map/substep/pallas_call | solution.py:506
  21.6 0.4 %collective-permute-start.5 = (f32[56,384]{1,0:T(8,128)S(1)}, f32[56,384]{1,0:T(8,128)S(1)}, u32[]{:S(2)}, u32[]{:S(2)}) collective-permute-start(f32[56,384]{1,0:T(8,128)S(1)} %get-tuple-element.70), channel_id=1, source_target_pairs={{0,1},{1,0},{2,3},{3,2},{4,5},{5,4},{6,7},{7,6},{8,9},{9,8},{10,11... | collective-permute-start | bytes 258056 | tf_op jit(solution)/shard_map/ppermute | solution.py:583
  22.1 0.9 %collective-permute-done.5.sibling = f32[56,384]{1,0:T(8,128)S(1)} collective-permute-done((f32[56,384]{1,0:T(8,128)S(1)}, f32[56,384]{1,0:T(8,128)S(1)}, u32[]{:S(2)}, u32[]{:S(2)}) %collective-permute-start.5) | collective-permute-done | bytes 86048 | tf_op jit(solution)/shard_map/ppermute | solution.py:583
  23.0 2.4 %collective-permute-start.6 = (f32[32,384]{1,0:T(8,128)S(1)}, f32[32,384]{1,0:T(8,128)S(1)}, u32[]{:S(2)}, u32[]{:S(2)}) collective-permute-start(f32[32,384]{1,0:T(8,128)S(1)} %pad_maximum_fusion.5), channel_id=1, source_target_pairs={{0,2},{1,0},{2,4},{3,1},{4,6},{5,3},{6,8},{7,5},{8,10},{9,7},{10,1... | collective-permute-start | bytes 147464 | tf_op jit(solution)/shard_map/ppermute | solution.py:533
  25.5 0.3 collective-permute-start.7
  25.7 0.6 %collective-permute-start.8 = (f32[32,384]{1,0:T(8,128)S(1)}, f32[32,384]{1,0:T(8,128)S(1)}, u32[]{:S(2)}, u32[]{:S(2)}) collective-permute-start(f32[32,384]{1,0:T(8,128)S(1)} %pad_maximum_fusion.7), channel_id=1, source_target_pairs={{0,6},{1,0},{2,8},{3,2},{4,10},{5,4},{6,12},{7,1},{8,14},{9,3},{10... | collective-permute-start | bytes 147464 | tf_op jit(solution)/shard_map/ppermute | solution.py:533
  26.3 2.6 %near_last.1 = (f32[24,1152]{1,0:T(8,128)S(1)}, f32[32,1152]{1,0:T(8,128)S(1)}, f32[4,8,1152]{2,1,0:T(8,128)S(1)}, f32[24,2304]{1,0:T(8,128)S(1)}, f32[32,2304]{...) custom-call(f32[56,384]{1,0:T(8,128)S(1)} %collective-permute-done.5.sibling, ...), custom_call_target="tpu_custom_call" | custom-call | flops 2000000000 | bytes 2000000 | tf_op jit(solution)/shard_map/near_last/pallas_call | solution.py:506
  28.9 0.0 collective-permute-done.6.got_1
  28.9 1.1 %collective-permute-done.7.got_2 = f32[32,384]{1,0:T(8,128)S(1)} collective-permute-done((f32[32,384]{1,0:T(8,128)S(1)}, f32[32,384]{1,0:T(8,128)S(1)}, u32[]{:S(2)}, u32[]{:S(2)}) %collective-permute-start.7) | collective-permute-done | bytes 49184 | tf_op jit(solution)/shard_map/ppermute | solution.py:533
  30.0 0.7 %collective-permute-done.8.got_3 = f32[32,384]{1,0:T(8,128)S(1)} collective-permute-done((f32[32,384]{1,0:T(8,128)S(1)}, f32[32,384]{1,0:T(8,128)S(1)}, u32[]{:S(2)}, u32[]{:S(2)}) %collective-permute-start.8) | collective-permute-done | bytes 49184 | tf_op jit(solution)/shard_map/ppermute | solution.py:533
  30.7 2.8 %collective-permute-start.9 = (f32[56,384]{1,0:T(8,128)S(1)}, f32[56,384]{1,0:T(8,128)S(1)}, u32[]{:S(2)}, u32[]{:S(2)}) collective-permute-start(f32[56,384]{1,0:T(8,128)S(1)} %pad_maximum_fusion.1), channel_id=1, source_target_pairs={{0,1},{1,0},{2,3},{3,2},{4,5},{5,4},{6,7},{7,6},{8,9},{9,8},{10,11... | collective-permute-start | bytes 258056 | tf_op jit(solution)/shard_map/ppermute | solution.py:535
  33.5 0.9 %collective-permute-done.9.back = f32[56,384]{1,0:T(8,128)S(1)} collective-permute-done((f32[56,384]{1,0:T(8,128)S(1)}, f32[56,384]{1,0:T(8,128)S(1)}, u32[]{:S(2)}, u32[]{:S(2)}) %collective-permute-start.9) | collective-permute-done | bytes 86048 | tf_op jit(solution)/shard_map/ppermute | solution.py:535
  34.5 2.5 %finish.1 = (f32[9,20,128]{2,1,0:T(8,128)}, f32[9,20,256]{2,1,0:T(8,128)}) custom-call(f32[32,384]{1,0:T(8,128)S(1)} %collective-permute-done.6.got_1, f32[32,384]{1,0:T(8,128)S(1)} %collective-permute-done.7.got_2, f32[32,384]{1,0:T(8,128)S(1)} %collective-permute-done.8.got_3, f32[56,384]{1,0:T(8,128)S(1)} %collective-permute-done.9.back, ...), custom_call_target="tpu_custom_call" | custom-call | flops 2000000000 | bytes 2000000 | tf_op jit(solution)/shard_map/finish/pallas_call | solution.py:506
  (18 shorter events, 0.1 us)
Async XLA Ops:
  5.0 1.7 %collective-permute-start = (f32[56,384]{1,0:T(8,128)S(1)}, f32[56,384]{1,0:T(8,128)S(1)}, u32[]{:S(2)}, u32[]{:S(2)}) collective-permute-start(f32[56,384]{1,0:T(8,128)S(1)} %get-tuple-element.48), channel_id=1, source_target_pairs={{0,1},{1,0},{2,3},{3,2},{4,5},{5,4},{6,7},{7,6},{8,9},{9,8},{10,11... | collective-permute-start | bytes 258056 | tf_op jit(solution)/shard_map/ppermute | solution.py:570
  6.7 7.3 %collective-permute-start.1 = (f32[32,384]{1,0:T(8,128)S(1)}, f32[32,384]{1,0:T(8,128)S(1)}, u32[]{:S(2)}, u32[]{:S(2)}) collective-permute-start(f32[32,384]{1,0:T(8,128)S(1)} %pad_maximum_fusion.2), channel_id=1, source_target_pairs={{0,2},{1,0},{2,4},{3,1},{4,6},{5,3},{6,8},{7,5},{8,10},{9,7},{10,1... | collective-permute-start | bytes 147464 | tf_op jit(solution)/shard_map/ppermute | solution.py:533
  11.6 4.7 %collective-permute-start.2 = (f32[32,384]{1,0:T(8,128)S(1)}, f32[32,384]{1,0:T(8,128)S(1)}, u32[]{:S(2)}, u32[]{:S(2)}) collective-permute-start(f32[32,384]{1,0:T(8,128)S(1)} %pad_maximum_fusion.3), channel_id=1, source_target_pairs={{0,4},{1,0},{2,6},{3,2},{4,8},{5,1},{6,10},{7,3},{8,12},{9,5},{10,... | collective-permute-start | bytes 147464 | tf_op jit(solution)/shard_map/ppermute | solution.py:533
  12.1 4.7 %collective-permute-start.3 = (f32[32,384]{1,0:T(8,128)S(1)}, f32[32,384]{1,0:T(8,128)S(1)}, u32[]{:S(2)}, u32[]{:S(2)}) collective-permute-start(f32[32,384]{1,0:T(8,128)S(1)} %pad_maximum_fusion.4), channel_id=1, source_target_pairs={{0,6},{1,0},{2,8},{3,2},{4,10},{5,4},{6,12},{7,1},{8,14},{9,3},{10... | collective-permute-start | bytes 147464 | tf_op jit(solution)/shard_map/ppermute | solution.py:533
  16.8 2.7 %collective-permute-start.4 = (f32[56,384]{1,0:T(8,128)S(1)}, f32[56,384]{1,0:T(8,128)S(1)}, u32[]{:S(2)}, u32[]{:S(2)}) collective-permute-start(f32[56,384]{1,0:T(8,128)S(1)} %pad_maximum_fusion), channel_id=1, source_target_pairs={{0,1},{1,0},{2,3},{3,2},{4,5},{5,4},{6,7},{7,6},{8,9},{9,8},{10,11... | collective-permute-start | bytes 258056 | tf_op jit(solution)/shard_map/ppermute | solution.py:535
  21.6 1.4 %collective-permute-start.5 = (f32[56,384]{1,0:T(8,128)S(1)}, f32[56,384]{1,0:T(8,128)S(1)}, u32[]{:S(2)}, u32[]{:S(2)}) collective-permute-start(f32[56,384]{1,0:T(8,128)S(1)} %get-tuple-element.70), channel_id=1, source_target_pairs={{0,1},{1,0},{2,3},{3,2},{4,5},{5,4},{6,7},{7,6},{8,9},{9,8},{10,11... | collective-permute-start | bytes 258056 | tf_op jit(solution)/shard_map/ppermute | solution.py:583
  23.0 5.9 %collective-permute-start.6 = (f32[32,384]{1,0:T(8,128)S(1)}, f32[32,384]{1,0:T(8,128)S(1)}, u32[]{:S(2)}, u32[]{:S(2)}) collective-permute-start(f32[32,384]{1,0:T(8,128)S(1)} %pad_maximum_fusion.5), channel_id=1, source_target_pairs={{0,2},{1,0},{2,4},{3,1},{4,6},{5,3},{6,8},{7,5},{8,10},{9,7},{10,1... | collective-permute-start | bytes 147464 | tf_op jit(solution)/shard_map/ppermute | solution.py:533
  25.5 4.6 %collective-permute-start.7 = (f32[32,384]{1,0:T(8,128)S(1)}, f32[32,384]{1,0:T(8,128)S(1)}, u32[]{:S(2)}, u32[]{:S(2)}) collective-permute-start(f32[32,384]{1,0:T(8,128)S(1)} %pad_maximum_fusion.6), channel_id=1, source_target_pairs={{0,4},{1,0},{2,6},{3,2},{4,8},{5,1},{6,10},{7,3},{8,12},{9,5},{10,... | collective-permute-start | bytes 147464 | tf_op jit(solution)/shard_map/ppermute | solution.py:533
  25.7 5.0 %collective-permute-start.8 = (f32[32,384]{1,0:T(8,128)S(1)}, f32[32,384]{1,0:T(8,128)S(1)}, u32[]{:S(2)}, u32[]{:S(2)}) collective-permute-start(f32[32,384]{1,0:T(8,128)S(1)} %pad_maximum_fusion.7), channel_id=1, source_target_pairs={{0,6},{1,0},{2,8},{3,2},{4,10},{5,4},{6,12},{7,1},{8,14},{9,3},{10... | collective-permute-start | bytes 147464 | tf_op jit(solution)/shard_map/ppermute | solution.py:533
  30.7 3.8 %collective-permute-start.9 = (f32[56,384]{1,0:T(8,128)S(1)}, f32[56,384]{1,0:T(8,128)S(1)}, u32[]{:S(2)}, u32[]{:S(2)}) collective-permute-start(f32[56,384]{1,0:T(8,128)S(1)} %pad_maximum_fusion.1), channel_id=1, source_target_pairs={{0,1},{1,0},{2,3},{3,2},{4,5},{5,4},{6,7},{7,6},{8,9},{9,8},{10,11... | collective-permute-start | bytes 258056 | tf_op jit(solution)/shard_map/ppermute | solution.py:535

commit v4 on v3

--- a/solution.py
+++ b/solution.py
@@ -359,12 +359,12 @@
                 l_ref[i * FP : (i + 1) * FP, p * LANES : (p + 1) * LANES] = acc[p]
         lifted = mm(w_lift, l_ref[...])
         base = get(base_ref, width, tile)
-        emit(tile, [base[p] + lifted[:, p * LANES : (p + 1) * LANES] for p in range(NQ)])
+        emit(tile, [base[p] + lifted[0:BP, p * LANES : (p + 1) * LANES] for p in range(NQ)], lifted)
 
 
 def near_fine_kernel(
-    sibling, x_fine, i_fine, c_first, star_f, flux_f, neighbors, faces, w_vol, w_proj,
-    base, side, near, p_own, p_coarse, spare,
+    sibling, x_fine, i_fine, c_first, star_f, flux_f, neighbors, faces, w_vol, w_proj, w_time, w_lift,
+    base, side, near, p_own, p_coarse, t_base, w_both, spare,
     t_ref,
 ):
     spare[...] = sibling[KEPT : KEPT + 8]
@@ -376,6 +376,14 @@
     near_part(
         x_fine, LANES, p_own, tables, neighbors, faces, star_f, flux_f, t_ref, base, side, near,
     )
+    w = weight(w_time, BP)
+    t_base[...] = mm(w, base[...])
+    hi, lo = halves(mm(w, w_lift[:, 0:32] + w_lift[:, 64:96]))
+    w_both[...] = jnp.zeros(w_both.shape, F32)
+    w_both[0:BP, :] = w_lift[...]
+    w_both[BP:, 0:32] = hi
+    w_both[BP:, 32:64] = hi
+    w_both[BP:, 64:96] = lo
 
 
 def near_last_kernel(
@@ -405,8 +413,8 @@
 
 
 def second_kernel(
-    got_1, got_2, got_3, back, sibling, x_fine, base, side, near, c_second, star_f, flux_f,
-    neighbors, faces, turns, send_fine, send_coarse, w_time, w_proj, w_rot, w_lift, count,
+    got_1, got_2, got_3, back, sibling, x_fine, base, side, near, t_base, c_second, star_f, flux_f,
+    neighbors, faces, turns, send_fine, send_coarse, w_time, w_proj, w_rot, w_both, count,
     keep, swap, x_next, i_next, p_gf, p_gc,
     ghost_f, ghost_c, t_ref, n_ref, l_ref, d_ref,
 ):
@@ -416,13 +424,14 @@
     p_gc[...] = mm(w_p, ghost_c[...])
     live = lax.broadcasted_iota(I32, (BP, LANES), 1) < count[0]
 
-    def emit_state(tile, values):
+    def emit_state(tile, values, lifted):
+        t_ref[...] = t_base[...] + lifted[BP:]
         old = get(x_fine, LANES, 0)
         put(x_next, [jnp.where(live, v, o) for v, o in zip(values, old)], LANES, 0)
 
     far_part(
         LANES, [(p_gf, LANES, 0), (p_gc, LANES, 0)], neighbors, faces, turns, flux_f,
-        w_rot, weight(w_lift, 32), base, side, near, n_ref, l_ref, emit_state,
+        w_rot, weight(w_both, 32), base, side, near, n_ref, l_ref, emit_state,
     )
 
     def emit_fine(tile, *terms):
@@ -430,7 +439,6 @@
         put(i_next, [jnp.where(live, v, 0.0) for v in values], LANES, 0)
 
     w = weight(w_time, BP)
-    t_ref[...] = mm(w, x_next[...])
     first_term(x_next, d_ref, t_ref, star_f, LANES)
     t_ref[...] = mm(w, d_ref[...])
     second_term(x_next, d_ref, t_ref, star_f, LANES, emit_fine)
@@ -451,7 +459,7 @@
     live = lax.broadcasted_iota(I32, (NB, LANES), 1) < count[0]
     ghosts = [(q_gf, LANES, 0), (q_gc, LANES, 0)]
 
-    def emit_fine(tile, values):
+    def emit_fine(tile, values, lifted):
         old = get(x_fine, LANES, 0)
         for p in range(NQ):
             fine_v[p] = jnp.where(live, values[p][:NB], old[p][:NB])
@@ -465,7 +473,7 @@
     q_gf[...] = q_gf[...] + p_gf[...]
     q_gc[...] = q_gc[...] + p_gc[...]
 
-    def emit_coarse(tile, values):
+    def emit_coarse(tile, values, lifted):
         for p in range(NQ):
             coarse_v[p, :, tile * LANES : (tile + 1) * LANES] = values[p][:NB]
 
@@ -568,17 +576,19 @@
     links, (w_time, *weights) = rest[:6], rest[6:]
     w_vol, w_proj, w_rot, w_lift = weights
     sibling = lax.ppermute(swap, "dom", SIBLING)
-    base, side, near, p_own, p_coarse, spare = call(
-        near_fine_kernel, "near_fine", [FINE, FACES_F, PICKED, FACES_F, FACES_C, (8, ROW)], [STIFF_F],
-        (sibling, x_fine, i_first, c_first, fine_star, fine_flux, *links[:2], w_vol, w_proj), (), us=1,
+    base, side, near, p_own, p_coarse, t_base, w_both, spare = call(
+        near_fine_kernel, "near_fine",
+        [FINE, FACES_F, PICKED, FACES_F, FACES_C, STIFF_F, (4 * BP, LANES), (8, ROW)], [STIFF_F],
+        (sibling, x_fine, i_first, c_first, fine_star, fine_flux, *links[:2], w_vol, w_proj,
+         w_time, w_lift), (), us=1,
     )
     arrived = exchange(keep, sibling, spare)
     keep, swap, x_next, i_second, p_gf, p_gc = call(
         second_kernel, "substep",
         [(KEPT, ROW), (KEPT + 8, ROW), FINE, FINE, FACES_F, FACES_G],
         [FINE, GHOST_C, STIFF_F, PICKED, FACES_F, FINE],
-        (*arrived, x_fine, base, side, near, c_second, fine_star, fine_flux, *links[:3],
-         send_fine, send_coarse, w_time, w_proj, w_rot, w_lift), count,
+        (*arrived, x_fine, base, side, near, t_base, c_second, fine_star, fine_flux, *links[:3],
+         send_fine, send_coarse, w_time, w_proj, w_rot, w_both), count,
     )
     sibling = lax.ppermute(swap, "dom", SIBLING)
     *near_parts, spare = call(

time: 37.2 us -> 36.9 us (level)
  the two profiles are of different devices: /device:TPU:97 before, /device:TPU:65 now
where the time goes in v4:
time: 36.9 us; the launch traced here: 36.8 us
  starting transfers between devices  15.1 us (41%)
  Pallas kernels  11.9 us (32%)
  waiting for transfers between devices  8.29 us (22%)
  between operations  1.37 us (4%)
    pallas_call x5, Pallas kernels, call(): pl.pallas_call(kernel, name=name, in_specs=[ANY if hbm_in else VM] * len(...  11.9 us
    ppermute x6, starting transfers between devices, exchange(): got[d] = lax.ppermute(sent[d], 'dom', ahead_by(d + 1))  8.82 us
    ppermute x2, starting transfers between devices, exchange(): back = lax.ppermute(jnp.concatenate(rest + [spare]), 'dom', SIBLING)  5.06 us
    ppermute x6, waiting for transfers between devices, exchange(): got[d] = lax.ppermute(sent[d], 'dom', ahead_by(d + 1))  4.59 us
    ppermute x2, waiting for transfers between devices, exchange(): back = lax.ppermute(jnp.concatenate(rest + [spare]), 'dom', SIBLING)  1.86 us
    ppermute x2, waiting for transfers between devices, local(): sibling = lax.ppermute(swap, 'dom', SIBLING)  1.84 us
    ppermute x2, starting transfers between devices, local(): sibling = lax.ppermute(swap, 'dom', SIBLING)  1.2 us
  transfers between devices with their start and end apart: 10, of which 8 were waited for; matrix products, arithmetic and copies ran while one was open for 0% of the time, Pallas kernels for 10%

profile of v4, /device:TPU:65, one launch (start us, length us, event | category | flops | bytes accessed | tf_op | source)
XLA Modules:
  0.0 36.8 jit_solution(11430269785015159457)
XLA Ops:
  1.3 3.6 %predict.1 = (f32[48,384]{1,0:T(8,128)S(1)}, f32[56,384]{1,0:T(8,128)S(1)}, f32[24,1152]{1,0:T(8,128)S(1)}, f32[24,1152]{1,0:T(8,128)S(1)}, f32[24,2304]{1,0:T(8...) custom-call(f32[9,20,128]{2,1,0:T(8,128)} %bitcast.41, ...), custom_call_target="tpu_custom_call" | custom-call | flops 2000000000 | bytes 2000000 | tf_op jit(solution)/shard_map/predict/pallas_call | solution.py:514
  4.9 0.8 %collective-permute-start = (f32[56,384]{1,0:T(8,128)S(1)}, f32[56,384]{1,0:T(8,128)S(1)}, u32[]{:S(2)}, u32[]{:S(2)}) collective-permute-start(f32[56,384]{1,0:T(8,128)S(1)} %get-tuple-element.50), channel_id=1, source_target_pairs={{0,1},{1,0},{2,3},{3,2},{4,5},{5,4},{6,7},{7,6},{8,9},{9,8},{10,11... | collective-permute-start | bytes 258056 | tf_op jit(solution)/shard_map/ppermute | solution.py:578
  5.7 0.9 %collective-permute-done.sibling = f32[56,384]{1,0:T(8,128)S(1)} collective-permute-done((f32[56,384]{1,0:T(8,128)S(1)}, f32[56,384]{1,0:T(8,128)S(1)}, u32[]{:S(2)}, u32[]{:S(2)}) %collective-permute-start) | collective-permute-done | bytes 86048 | tf_op jit(solution)/shard_map/ppermute | solution.py:578
  6.6 4.5 %collective-permute-start.1 = (f32[32,384]{1,0:T(8,128)S(1)}, f32[32,384]{1,0:T(8,128)S(1)}, u32[]{:S(2)}, u32[]{:S(2)}) collective-permute-start(f32[32,384]{1,0:T(8,128)S(1)} %pad_maximum_fusion.2), channel_id=1, source_target_pairs={{0,2},{1,0},{2,4},{3,1},{4,6},{5,3},{6,8},{7,5},{8,10},{9,7},{10,1... | collective-permute-start | bytes 147464 | tf_op jit(solution)/shard_map/ppermute | solution.py:541
  11.2 0.5 %collective-permute-start.2 = (f32[32,384]{1,0:T(8,128)S(1)}, f32[32,384]{1,0:T(8,128)S(1)}, u32[]{:S(2)}, u32[]{:S(2)}) collective-permute-start(f32[32,384]{1,0:T(8,128)S(1)} %pad_maximum_fusion.3), channel_id=1, source_target_pairs={{0,4},{1,0},{2,6},{3,2},{4,8},{5,1},{6,10},{7,3},{8,12},{9,5},{10,... | collective-permute-start | bytes 147464 | tf_op jit(solution)/shard_map/ppermute | solution.py:541
  11.7 0.8 %collective-permute-start.3 = (f32[32,384]{1,0:T(8,128)S(1)}, f32[32,384]{1,0:T(8,128)S(1)}, u32[]{:S(2)}, u32[]{:S(2)}) collective-permute-start(f32[32,384]{1,0:T(8,128)S(1)} %pad_maximum_fusion.4), channel_id=1, source_target_pairs={{0,6},{1,0},{2,8},{3,2},{4,10},{5,4},{6,12},{7,1},{8,14},{9,3},{10... | collective-permute-start | bytes 147464 | tf_op jit(solution)/shard_map/ppermute | solution.py:541
  12.5 1.3 %near_fine.1 = (f32[24,1152]{1,0:T(8,128)S(1)}, f32[32,1152]{1,0:T(8,128)S(1)}, f32[4,8,1152]{2,1,0:T(8,128)S(1)}, f32[32,1152]{1,0:T(8,128)S(1)}, f32[32,2304]{...) custom-call(f32[56,384]{1,0:T(8,128)S(1)} %collective-permute-done.sibling, ...), custom_call_target="tpu_custom_call" | custom-call | flops 1000000000 | bytes 1000000 | tf_op jit(solution)/shard_map/near_fine/pallas_call | solution.py:514
  13.8 0.0 collective-permute-done.1.got_1
  13.8 2.1 %collective-permute-done.2.got_2 = f32[32,384]{1,0:T(8,128)S(1)} collective-permute-done((f32[32,384]{1,0:T(8,128)S(1)}, f32[32,384]{1,0:T(8,128)S(1)}, u32[]{:S(2)}, u32[]{:S(2)}) %collective-permute-start.2) | collective-permute-done | bytes 49184 | tf_op jit(solution)/shard_map/ppermute | solution.py:541
  15.9 0.5 %collective-permute-done.3.got_3 = f32[32,384]{1,0:T(8,128)S(1)} collective-permute-done((f32[32,384]{1,0:T(8,128)S(1)}, f32[32,384]{1,0:T(8,128)S(1)}, u32[]{:S(2)}, u32[]{:S(2)}) %collective-permute-start.3) | collective-permute-done | bytes 49184 | tf_op jit(solution)/shard_map/ppermute | solution.py:541
  16.4 2.0 %collective-permute-start.4 = (f32[56,384]{1,0:T(8,128)S(1)}, f32[56,384]{1,0:T(8,128)S(1)}, u32[]{:S(2)}, u32[]{:S(2)}) collective-permute-start(f32[56,384]{1,0:T(8,128)S(1)} %pad_maximum_fusion), channel_id=1, source_target_pairs={{0,1},{1,0},{2,3},{3,2},{4,5},{5,4},{6,7},{7,6},{8,9},{9,8},{10,11... | collective-permute-start | bytes 258056 | tf_op jit(solution)/shard_map/ppermute | solution.py:543
  18.5 0.9 %collective-permute-done.4.back = f32[56,384]{1,0:T(8,128)S(1)} collective-permute-done((f32[56,384]{1,0:T(8,128)S(1)}, f32[56,384]{1,0:T(8,128)S(1)}, u32[]{:S(2)}, u32[]{:S(2)}) %collective-permute-start.4) | collective-permute-done | bytes 86048 | tf_op jit(solution)/shard_map/ppermute | solution.py:543
  19.4 2.0 %substep.1 = (f32[48,384]{1,0:T(8,128)S(1)}, f32[56,384]{1,0:T(8,128)S(1)}, f32[24,1152]{1,0:T(8,128)S(1)}, f32[24,1152]{1,0:T(8,128)S(1)}, f32[32,1152]{1,0:T(8,128)S(1)}, /*index=5*/f32[32,640]{1,0:T(8,128)S(1)}) custom-call(f32[32,384]{1,0:T(8,128)S(1)} %collective-permute-done.1.got_1, f32[32,384]{1,0:T(8,128)S(1)} %collective-permute-done.2.got_2, ...), custom_call_target="tpu_custom_call" | custom-call | flops 2000000000 | bytes 2000000 | tf_op jit(solution)/shard_map/substep/pallas_call | solution.py:514
  21.4 0.4 %collective-permute-start.5 = (f32[56,384]{1,0:T(8,128)S(1)}, f32[56,384]{1,0:T(8,128)S(1)}, u32[]{:S(2)}, u32[]{:S(2)}) collective-permute-start(f32[56,384]{1,0:T(8,128)S(1)} %get-tuple-element.74), channel_id=1, source_target_pairs={{0,1},{1,0},{2,3},{3,2},{4,5},{5,4},{6,7},{7,6},{8,9},{9,8},{10,11... | collective-permute-start | bytes 258056 | tf_op jit(solution)/shard_map/ppermute | solution.py:593
  21.8 0.9 %collective-permute-done.5.sibling = f32[56,384]{1,0:T(8,128)S(1)} collective-permute-done((f32[56,384]{1,0:T(8,128)S(1)}, f32[56,384]{1,0:T(8,128)S(1)}, u32[]{:S(2)}, u32[]{:S(2)}) %collective-permute-start.5) | collective-permute-done | bytes 86048 | tf_op jit(solution)/shard_map/ppermute | solution.py:593
  22.8 2.4 %collective-permute-start.6 = (f32[32,384]{1,0:T(8,128)S(1)}, f32[32,384]{1,0:T(8,128)S(1)}, u32[]{:S(2)}, u32[]{:S(2)}) collective-permute-start(f32[32,384]{1,0:T(8,128)S(1)} %pad_maximum_fusion.5), channel_id=1, source_target_pairs={{0,2},{1,0},{2,4},{3,1},{4,6},{5,3},{6,8},{7,5},{8,10},{9,7},{10,1... | collective-permute-start | bytes 147464 | tf_op jit(solution)/shard_map/ppermute | solution.py:541
  25.2 0.0 collective-permute-start.7
  25.2 0.5 %collective-permute-start.8 = (f32[32,384]{1,0:T(8,128)S(1)}, f32[32,384]{1,0:T(8,128)S(1)}, u32[]{:S(2)}, u32[]{:S(2)}) collective-permute-start(f32[32,384]{1,0:T(8,128)S(1)} %pad_maximum_fusion.7), channel_id=1, source_target_pairs={{0,6},{1,0},{2,8},{3,2},{4,10},{5,4},{6,12},{7,1},{8,14},{9,3},{10... | collective-permute-start | bytes 147464 | tf_op jit(solution)/shard_map/ppermute | solution.py:541
  25.8 2.5 %near_last.1 = (f32[24,1152]{1,0:T(8,128)S(1)}, f32[32,1152]{1,0:T(8,128)S(1)}, f32[4,8,1152]{2,1,0:T(8,128)S(1)}, f32[24,2304]{1,0:T(8,128)S(1)}, f32[32,2304]{...) custom-call(f32[56,384]{1,0:T(8,128)S(1)} %collective-permute-done.5.sibling, ...), custom_call_target="tpu_custom_call" | custom-call | flops 2000000000 | bytes 2000000 | tf_op jit(solution)/shard_map/near_last/pallas_call | solution.py:514
  28.3 0.0 collective-permute-done.6.got_1
  28.3 1.5 %collective-permute-done.7.got_2 = f32[32,384]{1,0:T(8,128)S(1)} collective-permute-done((f32[32,384]{1,0:T(8,128)S(1)}, f32[32,384]{1,0:T(8,128)S(1)}, u32[]{:S(2)}, u32[]{:S(2)}) %collective-permute-start.7) | collective-permute-done | bytes 49184 | tf_op jit(solution)/shard_map/ppermute | solution.py:541
  29.7 0.5 %collective-permute-done.8.got_3 = f32[32,384]{1,0:T(8,128)S(1)} collective-permute-done((f32[32,384]{1,0:T(8,128)S(1)}, f32[32,384]{1,0:T(8,128)S(1)}, u32[]{:S(2)}, u32[]{:S(2)}) %collective-permute-start.8) | collective-permute-done | bytes 49184 | tf_op jit(solution)/shard_map/ppermute | solution.py:541
  30.3 3.0 %collective-permute-start.9 = (f32[56,384]{1,0:T(8,128)S(1)}, f32[56,384]{1,0:T(8,128)S(1)}, u32[]{:S(2)}, u32[]{:S(2)}) collective-permute-start(f32[56,384]{1,0:T(8,128)S(1)} %pad_maximum_fusion.1), channel_id=1, source_target_pairs={{0,1},{1,0},{2,3},{3,2},{4,5},{5,4},{6,7},{7,6},{8,9},{9,8},{10,11... | collective-permute-start | bytes 258056 | tf_op jit(solution)/shard_map/ppermute | solution.py:543
  33.3 0.9 %collective-permute-done.9.back = f32[56,384]{1,0:T(8,128)S(1)} collective-permute-done((f32[56,384]{1,0:T(8,128)S(1)}, f32[56,384]{1,0:T(8,128)S(1)}, u32[]{:S(2)}, u32[]{:S(2)}) %collective-permute-start.9) | collective-permute-done | bytes 86048 | tf_op jit(solution)/shard_map/ppermute | solution.py:543
  34.2 2.5 %finish.1 = (f32[9,20,128]{2,1,0:T(8,128)}, f32[9,20,256]{2,1,0:T(8,128)}) custom-call(f32[32,384]{1,0:T(8,128)S(1)} %collective-permute-done.6.got_1, f32[32,384]{1,0:T(8,128)S(1)} %collective-permute-done.7.got_2, f32[32,384]{1,0:T(8,128)S(1)} %collective-permute-done.8.got_3, f32[56,384]{1,0:T(8,128)S(1)} %collective-permute-done.9.back, ...), custom_call_target="tpu_custom_call" | custom-call | flops 2000000000 | bytes 2000000 | tf_op jit(solution)/shard_map/finish/pallas_call | solution.py:514
  (18 shorter events, 0.1 us)
Async XLA Ops:
  4.9 1.7 %collective-permute-start = (f32[56,384]{1,0:T(8,128)S(1)}, f32[56,384]{1,0:T(8,128)S(1)}, u32[]{:S(2)}, u32[]{:S(2)}) collective-permute-start(f32[56,384]{1,0:T(8,128)S(1)} %get-tuple-element.50), channel_id=1, source_target_pairs={{0,1},{1,0},{2,3},{3,2},{4,5},{5,4},{6,7},{7,6},{8,9},{9,8},{10,11... | collective-permute-start | bytes 258056 | tf_op jit(solution)/shard_map/ppermute | solution.py:578
  6.6 7.2 %collective-permute-start.1 = (f32[32,384]{1,0:T(8,128)S(1)}, f32[32,384]{1,0:T(8,128)S(1)}, u32[]{:S(2)}, u32[]{:S(2)}) collective-permute-start(f32[32,384]{1,0:T(8,128)S(1)} %pad_maximum_fusion.2), channel_id=1, source_target_pairs={{0,2},{1,0},{2,4},{3,1},{4,6},{5,3},{6,8},{7,5},{8,10},{9,7},{10,1... | collective-permute-start | bytes 147464 | tf_op jit(solution)/shard_map/ppermute | solution.py:541
  11.2 4.7 %collective-permute-start.2 = (f32[32,384]{1,0:T(8,128)S(1)}, f32[32,384]{1,0:T(8,128)S(1)}, u32[]{:S(2)}, u32[]{:S(2)}) collective-permute-start(f32[32,384]{1,0:T(8,128)S(1)} %pad_maximum_fusion.3), channel_id=1, source_target_pairs={{0,4},{1,0},{2,6},{3,2},{4,8},{5,1},{6,10},{7,3},{8,12},{9,5},{10,... | collective-permute-start | bytes 147464 | tf_op jit(solution)/shard_map/ppermute | solution.py:541
  11.7 4.7 %collective-permute-start.3 = (f32[32,384]{1,0:T(8,128)S(1)}, f32[32,384]{1,0:T(8,128)S(1)}, u32[]{:S(2)}, u32[]{:S(2)}) collective-permute-start(f32[32,384]{1,0:T(8,128)S(1)} %pad_maximum_fusion.4), channel_id=1, source_target_pairs={{0,6},{1,0},{2,8},{3,2},{4,10},{5,4},{6,12},{7,1},{8,14},{9,3},{10... | collective-permute-start | bytes 147464 | tf_op jit(solution)/shard_map/ppermute | solution.py:541
  16.4 3.0 %collective-permute-start.4 = (f32[56,384]{1,0:T(8,128)S(1)}, f32[56,384]{1,0:T(8,128)S(1)}, u32[]{:S(2)}, u32[]{:S(2)}) collective-permute-start(f32[56,384]{1,0:T(8,128)S(1)} %pad_maximum_fusion), channel_id=1, source_target_pairs={{0,1},{1,0},{2,3},{3,2},{4,5},{5,4},{6,7},{7,6},{8,9},{9,8},{10,11... | collective-permute-start | bytes 258056 | tf_op jit(solution)/shard_map/ppermute | solution.py:543
  21.4 1.4 %collective-permute-start.5 = (f32[56,384]{1,0:T(8,128)S(1)}, f32[56,384]{1,0:T(8,128)S(1)}, u32[]{:S(2)}, u32[]{:S(2)}) collective-permute-start(f32[56,384]{1,0:T(8,128)S(1)} %get-tuple-element.74), channel_id=1, source_target_pairs={{0,1},{1,0},{2,3},{3,2},{4,5},{5,4},{6,7},{7,6},{8,9},{9,8},{10,11... | collective-permute-start | bytes 258056 | tf_op jit(solution)/shard_map/ppermute | solution.py:593
  22.8 5.5 %collective-permute-start.6 = (f32[32,384]{1,0:T(8,128)S(1)}, f32[32,384]{1,0:T(8,128)S(1)}, u32[]{:S(2)}, u32[]{:S(2)}) collective-permute-start(f32[32,384]{1,0:T(8,128)S(1)} %pad_maximum_fusion.5), channel_id=1, source_target_pairs={{0,2},{1,0},{2,4},{3,1},{4,6},{5,3},{6,8},{7,5},{8,10},{9,7},{10,1... | collective-permute-start | bytes 147464 | tf_op jit(solution)/shard_map/ppermute | solution.py:541
  25.2 4.6 %collective-permute-start.7 = (f32[32,384]{1,0:T(8,128)S(1)}, f32[32,384]{1,0:T(8,128)S(1)}, u32[]{:S(2)}, u32[]{:S(2)}) collective-permute-start(f32[32,384]{1,0:T(8,128)S(1)} %pad_maximum_fusion.6), channel_id=1, source_target_pairs={{0,4},{1,0},{2,6},{3,2},{4,8},{5,1},{6,10},{7,3},{8,12},{9,5},{10,... | collective-permute-start | bytes 147464 | tf_op jit(solution)/shard_map/ppermute | solution.py:541
  25.2 5.0 %collective-permute-start.8 = (f32[32,384]{1,0:T(8,128)S(1)}, f32[32,384]{1,0:T(8,128)S(1)}, u32[]{:S(2)}, u32[]{:S(2)}) collective-permute-start(f32[32,384]{1,0:T(8,128)S(1)} %pad_maximum_fusion.7), channel_id=1, source_target_pairs={{0,6},{1,0},{2,8},{3,2},{4,10},{5,4},{6,12},{7,1},{8,14},{9,3},{10... | collective-permute-start | bytes 147464 | tf_op jit(solution)/shard_map/ppermute | solution.py:541
  30.3 4.0 %collective-permute-start.9 = (f32[56,384]{1,0:T(8,128)S(1)}, f32[56,384]{1,0:T(8,128)S(1)}, u32[]{:S(2)}, u32[]{:S(2)}) collective-permute-start(f32[56,384]{1,0:T(8,128)S(1)} %pad_maximum_fusion.1), channel_id=1, source_target_pairs={{0,1},{1,0},{2,3},{3,2},{4,5},{5,4},{6,7},{7,6},{8,9},{9,8},{10,11... | collective-permute-start | bytes 258056 | tf_op jit(solution)/shard_map/ppermute | solution.py:543
